TPU v7x, 32 devices: a whole 2x2x4 slice. The times are simulated.
32 devices in a mesh: parts: 2 (over x), shift: 16 (over z, y, core).
Axes of the slice: x: 2, y: 2, z: 4, core: 2. Of those that a mesh axis runs over, the one named last changes fastest.
Arguments:
- embeddings: bfloat16 [16384, 768], P(('parts', 'shift')), parts along dimension 0, as said below
- block_cluster: int32 [128], P(('parts', 'shift')), parts along dimension 0, may hold values from 0 to 7, never falling along the last dimension, each value on 1 to 16 neighbouring positions
Outputs:
- best_match: float32 [16384], P(('parts', 'shift')), parts along dimension 0
There are 2 independent parts, one for each index of `parts`. A program takes and returns all parts, laid end to end along the dimension named above; each array names one. Nothing has to cross between parts.
Inputs may be any that keep to these rules, and one draw needn't show every extreme that they name: block_cluster never falls along the blocks; each cluster holds 1 to 16 consecutive blocks and one holds exactly 16. `embeddings`: every row is nonzero; rows may differ in scale, which the first step removes.
All inputs are finite; a program needn't handle non-finite values.
Results may differ from a plain program's by a relative error of at most 0.00059.
Values may be sent and summed in bfloat16 or wider, within the bound.
No kernel may reach another device: no remote copies, remote signals or barrier semaphores. Data moves between devices by JAX's collectives and lax.ppermute only.
A program may use at most 64 MiB of HBM per device.

v0:
```python
import math

import jax
import jax.numpy as jnp
from jax import lax
from jax.experimental import pallas as pl
from jax.experimental.pallas import tpu as pltpu
from jax.sharding import PartitionSpec as P

LOW = -2.0
QUAD = 4
BLOCK = 128
LANES = 128
PAD = 16


def swapped(array, mask):
    length = lax.axis_size("shift")
    return lax.ppermute(array, "shift", [(i, i ^ mask) for i in range(length)])


def next_quad():
    parts, count = lax.axis_size("parts"), lax.axis_size("shift")
    pairs = []
    for part in range(parts):
        by = QUAD if part % 2 == 0 else -QUAD
        for i in range(count):
            there = i + by
            if 0 <= there < count:
                pairs.append((part * count + i, part * count + there))
            elif part ^ 1 < parts:
                pairs.append((part * count + i, (part ^ 1) * count + i))
    return pairs


def forward(array):
    return lax.ppermute(array, ("parts", "shift"), next_quad())


def backward(array):
    return lax.ppermute(array, ("parts", "shift"), [(b, a) for a, b in next_quad()])


def unit_rows(raw):
    values = raw.astype(jnp.float32)
    scale = lax.rsqrt(jnp.mean(values * values, axis=1, keepdims=True) + 1e-06) / math.sqrt(
        raw.shape[1]
    )
    return (values * scale).astype(jnp.bfloat16)


def product(rows, columns):
    return lax.dot_general(
        rows, columns, (((1,), (1,)), ((), ())), preferred_element_type=jnp.float32
    )


def ids_of(packet, valid=None):
    blocks = packet.shape[0] - PAD
    values = packet[blocks:, :LANES].astype(jnp.float32)
    if valid is not None:
        values = jnp.where(valid[0] != 0, values, -1.0)
    count = blocks // BLOCK
    return [jnp.broadcast_to(values[b : b + 1], (8, LANES)) for b in range(count)]


def shares(p, q):
    meet = jnp.logical_and(p[0] <= q[-1], q[0] <= p[-1])
    return jnp.max(jnp.where(meet, 1.0, 0.0)) > 0.0


def tile_of(sims, a, b):
    tile = sims[a * BLOCK : (a + 1) * BLOCK, b * BLOCK : (b + 1) * BLOCK]
    return tile.reshape(BLOCK // 8, 8, BLOCK)


def column_best(p, q, sims, own=False):
    pieces = []
    for b in range(len(q)):
        top = jnp.full((8, BLOCK), LOW, jnp.float32)
        for a in range(len(p)):
            tile = tile_of(sims, a, b)
            if own and a == b:
                row = lax.broadcasted_iota(jnp.int32, tile.shape, 0) * 8 + (
                    lax.broadcasted_iota(jnp.int32, tile.shape, 1)
                )
                tile = jnp.where(row == lax.broadcasted_iota(jnp.int32, tile.shape, 2), LOW, tile)
            top = jnp.maximum(top, jnp.where(p[a] == q[b], jnp.max(tile, axis=0), LOW))
        pieces.append(jnp.max(top, axis=0, keepdims=True))
    return jnp.concatenate(pieces, axis=1)


def row_best(p, q, sims):
    pieces = []
    for a in range(len(p)):
        top = jnp.full((BLOCK // 8, 8, BLOCK), LOW, jnp.float32)
        for b in range(len(q)):
            shift = jnp.where(p[a] == q[b], 0.0, -4.0)
            top = jnp.maximum(top, tile_of(sims, a, b) + shift[None])
        pieces.append(jnp.max(top.reshape(BLOCK, BLOCK).T, axis=0, keepdims=True))
    return jnp.concatenate(pieces, axis=1)


def rows_of(packet):
    return packet[: packet.shape[0] - PAD, :]


def packet_kernel(ids_hbm, own_hbm, packet, held, own_ids, sems, ids_sem):
    rows, depth = held.shape
    count = rows // BLOCK
    copies = []
    ids_copy = pltpu.make_async_copy(ids_hbm, own_ids, ids_sem)
    ids_copy.start()
    for b in range(count):
        part = pl.ds(b * BLOCK, BLOCK)
        copies.append(pltpu.make_async_copy(own_hbm.at[part], held.at[part], sems.at[b]))
        copies[b].start()
    for b in range(count):
        copies[b].wait()
        part = pl.ds(b * BLOCK, BLOCK)
        packet[part, :] = unit_rows(held[part, :])
    ids_copy.wait()
    row = lax.broadcasted_iota(jnp.int32, (PAD, depth), 0)
    ids = jnp.full((PAD, depth), -1.0, jnp.float32)
    for b in range(count):
        ids = jnp.where(row == b, own_ids[b].astype(jnp.float32), ids)
    packet[rows:, :] = ids.astype(jnp.bfloat16)


def near_kernel(own_ref, mate_ref, best):
    own, mate = ids_of(own_ref), ids_of(mate_ref)
    best[...] = column_best(own, own, product(rows_of(own_ref), rows_of(own_ref)), own=True)

    @pl.when(shares(mate, own))
    def _():
        sims = product(rows_of(mate_ref), rows_of(own_ref))
        best[...] = jnp.maximum(best[...], column_best(mate, own, sims))


def partner_kernel(own_ref, partner_ref, best_in, best):
    own, partner = ids_of(own_ref), ids_of(partner_ref)
    best[...] = best_in[...]

    @pl.when(shares(partner, own))
    def _():
        sims = product(rows_of(partner_ref), rows_of(own_ref))
        best[...] = jnp.maximum(best[...], column_best(partner, own, sims))


def first_kernel(
    valid, own_ref, mate_ref, cross_ref, back_ref, best_in, best, to_mate, back
):
    own, mate, cross = ids_of(own_ref), ids_of(mate_ref), ids_of(cross_ref)
    behind = ids_of(back_ref, valid)
    best[...] = best_in[...]
    back[...] = jnp.full_like(back, LOW)
    to_mate[...] = jnp.full_like(to_mate, LOW)
    hits = [shares(mate, behind), shares(cross, behind), shares(cross, own)]

    for row, (ids, held) in enumerate(((mate, mate_ref), (cross, cross_ref))):

        @pl.when(hits[row])
        def _(row=row, ids=ids, held=held):
            sims = product(rows_of(held), rows_of(back_ref))
            back[...] = jnp.maximum(back[...], column_best(ids, behind, sims))
            to_mate[row : row + 1, :] = row_best(ids, behind, sims)

    @pl.when(hits[2])
    def _():
        sims = product(rows_of(cross_ref), rows_of(own_ref))
        best[...] = jnp.maximum(best[...], column_best(cross, own, sims))


def second_kernel(
    valid, own_ref, partner_ref, back_ref, best_in, back_in, best, to_partner, back
):
    own, partner = ids_of(own_ref), ids_of(partner_ref)
    behind = ids_of(back_ref, valid)
    best[...] = best_in[...]
    back[...] = back_in[...]
    to_partner[...] = jnp.full_like(to_partner, LOW)
    hits = [shares(own, behind), shares(partner, behind)]

    @pl.when(hits[0])
    def _():
        sims = product(rows_of(own_ref), rows_of(back_ref))
        back[...] = jnp.maximum(back[...], column_best(own, behind, sims))
        best[...] = jnp.maximum(best[...], row_best(own, behind, sims))

    @pl.when(hits[1])
    def _():
        sims = product(rows_of(partner_ref), rows_of(back_ref))
        back[...] = jnp.maximum(back[...], column_best(partner, behind, sims))
        to_partner[...] = row_best(partner, behind, sims)


def local(embeddings, block_cluster):
    rows, depth = embeddings.shape
    count = lax.axis_size("shift")
    mine = lax.axis_index("shift")
    upward = lax.axis_index("parts") % 2 == 0
    has_quad_below = mine >= QUAD
    has_quad_above = mine + QUAD < count
    receives = jnp.where(upward, has_quad_below, has_quad_above)
    returns = jnp.where(upward, has_quad_above, has_quad_below)
    valid = receives.astype(jnp.int32).reshape(1)

    smem = pl.BlockSpec(memory_space=pltpu.SMEM)
    vmem = pl.BlockSpec(memory_space=pltpu.VMEM)
    line = jax.ShapeDtypeStruct((1, rows), jnp.float32)
    lines = jax.ShapeDtypeStruct((2, rows), jnp.float32)

    def call(kernel, products, outs, specs, inputs, scratch=(), limit=40):
        return pl.pallas_call(
            kernel,
            out_shape=outs,
            in_specs=specs + [vmem] * (len(inputs) - len(specs)),
            out_specs=(vmem,) * len(outs),
            scratch_shapes=scratch,
            compiler_params=pltpu.CompilerParams(vmem_limit_bytes=limit * 1024 * 1024),
            cost_estimate=pl.CostEstimate(
                flops=2 * products * rows * rows * depth,
                bytes_accessed=2 * rows * depth,
                transcendentals=0,
            ),
        )(*inputs)

    (packet,) = call(
        packet_kernel, 0, (jax.ShapeDtypeStruct((rows + PAD, depth), jnp.bfloat16),),
        [pl.BlockSpec(memory_space=pltpu.HBM)] * 2,
        tuple(pltpu.with_memory_space_constraint(a, pltpu.HBM) for a in (block_cluster, embeddings)),
        (
            pltpu.VMEM((rows, depth), jnp.bfloat16),
            pltpu.SMEM(block_cluster.shape, jnp.int32),
            pltpu.SemaphoreType.DMA((rows // BLOCK,)),
            pltpu.SemaphoreType.DMA,
        ),
    )
    partner = swapped(packet, 2)
    behind = forward(packet)
    mate = swapped(packet, 1)
    (best,) = call(near_kernel, 0, (line,), [], (packet, mate))
    partner, best = lax.optimization_barrier((partner, best))
    cross = swapped(partner, 1)
    (best,) = call(partner_kernel, 0, (line,), [], (packet, partner, best))
    best, to_mate, back = call(
        first_kernel, 3, (line, lines, line), [smem], (valid, packet, mate, cross, behind, best)
    )
    from_mate = swapped(to_mate, 1)
    best, to_partner, back = call(
        second_kernel, 2, (line, line, line), [smem], (valid, packet, partner, behind, best, back)
    )
    from_next = jnp.where(returns, backward(back), LOW)
    from_partner = swapped(jnp.maximum(to_partner, from_mate[1:2]), 2)
    best = jnp.maximum(jnp.maximum(best, from_next), jnp.maximum(from_mate[0:1], from_partner))
    return jnp.maximum(best.reshape(rows), -1.0)


def solution(mesh):
    return jax.shard_map(
        local,
        mesh=mesh,
        in_specs=(P(("parts", "shift"), None), P(("parts", "shift"))),
        out_specs=P(("parts", "shift")),
        check_vma=False,
    )
```

profile of v0, /device:TPU:0, one launch (start us, length us, event | category | flops | bytes accessed | tf_op | source)
XLA Modules:
  0.0 34.6 jit_solution(4995453713689169512)
XLA Ops:
  0.0 1.5 %shard_map.28.own_ref = bf16[528,768]{1,0:T(8,128)(2,1)S(1)} custom-call(s32[4]{0:T(128)} %ids_hbm.1, bf16[512,768]{1,0:T(8,128)(2,1)} %own_hbm.1), custom_call_target="tpu_custom_call" | custom-call | bytes 786432 | tf_op jit(solution)/shard_map/pallas_call | solution.py:214
  1.5 0.5 %collective-permute-start.1 = (bf16[528,768]{1,0:T(8,128)(2,1)S(1)}, bf16[528,768]{1,0:T(8,128)(2,1)S(1)}, u32[]{:S(2)}, u32[]{:S(2)}) collective-permute-start(bf16[528,768]{1,0:T(8,128)(2,1)S(1)} %shard_map.28.own_ref), channel_id=1, source_target_pairs={{0,1},{1,0},{2,3},{3,2},{4,5},{5,4},{6,7},{7,6},{8,9},{9,8},{10,11... | collective-permute-start | bytes 2433032 | tf_op jit(solution)/shard_map/ppermute | solution.py:19
  2.0 2.6 %collective-permute-start = (bf16[528,768]{1,0:T(8,128)(2,1)S(1)}, bf16[528,768]{1,0:T(8,128)(2,1)S(1)}, u32[]{:S(2)}, u32[]{:S(2)}) collective-permute-start(bf16[528,768]{1,0:T(8,128)(2,1)S(1)} %shard_map.28.own_ref), channel_id=1, source_target_pairs={{0,2},{1,3},{2,0},{3,1},{4,6},{5,7},{6,4},{7,5},{8,10},{9,11},{10,... | collective-permute-start | bytes 2433032 | tf_op jit(solution)/shard_map/ppermute | solution.py:19
  4.6 1.6 %collective-permute-start.2 = (bf16[528,768]{1,0:T(8,128)(2,1)S(1)}, bf16[528,768]{1,0:T(8,128)(2,1)S(1)}, u32[]{:S(2)}, u32[]{:S(2)}) collective-permute-start(bf16[528,768]{1,0:T(8,128)(2,1)S(1)} %shard_map.28.own_ref), channel_id=1, source_target_pairs={{0,4},{1,5},{2,6},{3,7},{4,8},{5,9},{6,10},{7,11},{8,12},{9,13},{1... | collective-permute-start | bytes 2433032 | tf_op jit(solution)/shard_map/ppermute | solution.py:37
  6.2 0.0 collective-permute-done.1.mate_ref
  6.2 1.2 %shard_map.29.best_in = f32[1,512]{1,0:T(1,128)S(1)} custom-call(bf16[528,768]{1,0:T(8,128)(2,1)S(1)} %shard_map.28.own_ref, bf16[528,768]{1,0:T(8,128)(2,1)S(1)} %collective-permute-done.1.mate_ref), custom_call_target="tpu_custom_call" | custom-call | bytes 786432 | tf_op jit(solution)/shard_map/pallas_call | solution.py:214
  7.4 15.8 %collective-permute-done.partner_ref = bf16[528,768]{1,0:T(8,128)(2,1)S(1)} collective-permute-done((bf16[528,768]{1,0:T(8,128)(2,1)S(1)}, bf16[528,768]{1,0:T(8,128)(2,1)S(1)}, u32[]{:S(2)}, u32[]{:S(2)}) %collective-permute-start) | collective-permute-done | bytes 811040 | tf_op jit(solution)/shard_map/ppermute | solution.py:19
  23.3 0.0 collective-permute-start.3
  23.3 0.7 %shard_map.30.best_in = f32[1,512]{1,0:T(1,128)S(1)} custom-call(bf16[528,768]{1,0:T(8,128)(2,1)S(1)} %shard_map.28.own_ref, bf16[528,768]{1,0:T(8,128)(2,1)S(1)} %collective-permute-done.partner_ref, f32[1,512]{1,0:T(1,128)S(1)} %shard_map.29.best_in), custom_call_target="tpu_custom_call" | custom-call | bytes 786432 | tf_op jit(solution)/shard_map/pallas_call | solution.py:214
  24.0 0.7 %collective-permute-done.2.back_ref = bf16[528,768]{1,0:T(8,128)(2,1)S(1)} collective-permute-done((bf16[528,768]{1,0:T(8,128)(2,1)S(1)}, bf16[528,768]{1,0:T(8,128)(2,1)S(1)}, u32[]{:S(2)}, u32[]{:S(2)}) %collective-permute-start.2) | collective-permute-done | bytes 811040 | tf_op jit(solution)/shard_map/ppermute | solution.py:37
  24.8 1.0 %collective-permute-done.3.cross_ref = bf16[528,768]{1,0:T(8,128)(2,1)} collective-permute-done((bf16[528,768]{1,0:T(8,128)(2,1)S(1)}, bf16[528,768]{1,0:T(8,128)(2,1)}, u32[]{:S(2)}, u32[]{:S(2)}) %collective-permute-start.3) | collective-permute-done | bytes 811040 | tf_op jit(solution)/shard_map/ppermute | solution.py:19
  25.7 1.3 %shard_map.31 = (f32[1,512]{1,0:T(1,128)S(1)}, f32[2,512]{1,0:T(2,128)S(1)}, f32[1,512]{1,0:T(1,128)S(1)}) custom-call(s32[1]{0:T(128)} %bitcast.valid, bf16[528,768]{1,0:T(8,128)(2,1)S(1)} %shard_map.28.own_ref, bf16[528,768]{1,0:T(8,128)(2,1)S(1)} %collective-permute-done.1.mate_ref, bf16[528,768]{1,0:T(8,128)(2,1)} %collective-permute-done.3.cross_ref, ...), custom_call_target="tpu_custom_call" | custom-call | flops 1207959552 | bytes 786432 | tf_op jit(solution)/shard_map/pallas_call | solution.py:214
  27.0 0.8 %collective-permute-start.5 = (f32[2,512]{1,0:T(2,128)S(1)}, f32[2,512]{1,0:T(2,128)S(1)}, u32[]{:S(2)}, u32[]{:S(2)}) collective-permute-start(f32[2,512]{1,0:T(2,128)S(1)} %get-tuple-element.19), channel_id=1, source_target_pairs={{0,1},{1,0},{2,3},{3,2},{4,5},{5,4},{6,7},{7,6},{8,9},{9,8},{10,11... | collective-permute-start | bytes 12296 | tf_op jit(solution)/shard_map/ppermute | solution.py:19
  27.8 0.1 shard_map.32
  28.0 2.3 %collective-permute-start.4 = (f32[1,512]{1,0:T(1,128)S(1)}, f32[1,512]{1,0:T(1,128)S(1)}, u32[]{:S(2)}, u32[]{:S(2)}) collective-permute-start(f32[1,512]{1,0:T(1,128)S(1)} %get-tuple-element.18), channel_id=1, source_target_pairs={{4,0},{5,1},{6,2},{7,3},{8,4},{9,5},{10,6},{11,7},{12,8},{13,9},{1... | collective-permute-start | bytes 6152 | tf_op jit(solution)/shard_map/ppermute | solution.py:41
  30.3 0.0 collective-permute-done.5
  30.3 1.0 %collective-permute-start.6 = (f32[1,512]{1,0:T(1,128)S(1)}, f32[1,512]{1,0:T(1,128)S(1)}, u32[]{:S(2)}, u32[]{:S(2)}) collective-permute-start(f32[1,512]{1,0:T(1,128)S(1)} %slice_maximum_fusion), channel_id=1, source_target_pairs={{0,2},{1,3},{2,0},{3,1},{4,6},{5,7},{6,4},{7,5},{8,10},{9,11},{10,... | collective-permute-start | bytes 6152 | tf_op jit(solution)/shard_map/ppermute | solution.py:19
  31.4 0.3 collective-permute-done.4
  31.6 2.4 %collective-permute-done.6 = f32[1,512]{1,0:T(1,128)S(1)} collective-permute-done((f32[1,512]{1,0:T(1,128)S(1)}, f32[1,512]{1,0:T(1,128)S(1)}, u32[]{:S(2)}, u32[]{:S(2)}) %collective-permute-start.6) | collective-permute-done | bytes 2080 | tf_op jit(solution)/shard_map/ppermute | solution.py:19
  34.0 0.6 %fusion.2 = f32[1,512]{1,0:T(1,128)} fusion(f32[1,512]{1,0:T(1,128)S(1)} %collective-permute-done.6, f32[2,512]{1,0:T(2,128)S(1)} %collective-permute-done.5, f32[1,512]{1,0:T(1,128)S(1)} %get-tuple-element.17, f32[1,512]{1,0:T(1,128)S(1)} %collective-permute-done.4, pred[]{:T(512)S(6)} %select_n.24), kind=kLoop, calls=%fused_computation.5 | loop fusion | flops 2560 | bytes 10241 | tf_op jit(solution)/shard_map/max | solution.py:256
  (1 shorter events, 0.0 us)
Async XLA Ops:
  1.5 4.7 %collective-permute-start.1 = (bf16[528,768]{1,0:T(8,128)(2,1)S(1)}, bf16[528,768]{1,0:T(8,128)(2,1)S(1)}, u32[]{:S(2)}, u32[]{:S(2)}) collective-permute-start(bf16[528,768]{1,0:T(8,128)(2,1)S(1)} %shard_map.28.own_ref), channel_id=1, source_target_pairs={{0,1},{1,0},{2,3},{3,2},{4,5},{5,4},{6,7},{7,6},{8,9},{9,8},{10,11... | collective-permute-start | bytes 2433032 | tf_op jit(solution)/shard_map/ppermute | solution.py:19
  2.0 21.3 %collective-permute-start = (bf16[528,768]{1,0:T(8,128)(2,1)S(1)}, bf16[528,768]{1,0:T(8,128)(2,1)S(1)}, u32[]{:S(2)}, u32[]{:S(2)}) collective-permute-start(bf16[528,768]{1,0:T(8,128)(2,1)S(1)} %shard_map.28.own_ref), channel_id=1, source_target_pairs={{0,2},{1,3},{2,0},{3,1},{4,6},{5,7},{6,4},{7,5},{8,10},{9,11},{10,... | collective-permute-start | bytes 2433032 | tf_op jit(solution)/shard_map/ppermute | solution.py:19
  4.6 20.1 %collective-permute-start.2 = (bf16[528,768]{1,0:T(8,128)(2,1)S(1)}, bf16[528,768]{1,0:T(8,128)(2,1)S(1)}, u32[]{:S(2)}, u32[]{:S(2)}) collective-permute-start(bf16[528,768]{1,0:T(8,128)(2,1)S(1)} %shard_map.28.own_ref), channel_id=1, source_target_pairs={{0,4},{1,5},{2,6},{3,7},{4,8},{5,9},{6,10},{7,11},{8,12},{9,13},{1... | collective-permute-start | bytes 2433032 | tf_op jit(solution)/shard_map/ppermute | solution.py:37
  23.3 2.5 %collective-permute-start.3 = (bf16[528,768]{1,0:T(8,128)(2,1)S(1)}, bf16[528,768]{1,0:T(8,128)(2,1)}, u32[]{:S(2)}, u32[]{:S(2)}) collective-permute-start(bf16[528,768]{1,0:T(8,128)(2,1)S(1)} %collective-permute-done.partner_ref), channel_id=1, source_target_pairs={{0,1},{1,0},{2,3},{3,2},{4,5},{5,4},{6,7},{7,6},{8,9},{9,8},{10,11... | collective-permute-start | bytes 2433032 | tf_op jit(solution)/shard_map/ppermute | solution.py:19
  27.0 3.3 %collective-permute-start.5 = (f32[2,512]{1,0:T(2,128)S(1)}, f32[2,512]{1,0:T(2,128)S(1)}, u32[]{:S(2)}, u32[]{:S(2)}) collective-permute-start(f32[2,512]{1,0:T(2,128)S(1)} %get-tuple-element.19), channel_id=1, source_target_pairs={{0,1},{1,0},{2,3},{3,2},{4,5},{5,4},{6,7},{7,6},{8,9},{9,8},{10,11... | collective-permute-start | bytes 12296 | tf_op jit(solution)/shard_map/ppermute | solution.py:19
  28.0 3.7 %collective-permute-start.4 = (f32[1,512]{1,0:T(1,128)S(1)}, f32[1,512]{1,0:T(1,128)S(1)}, u32[]{:S(2)}, u32[]{:S(2)}) collective-permute-start(f32[1,512]{1,0:T(1,128)S(1)} %get-tuple-element.18), channel_id=1, source_target_pairs={{4,0},{5,1},{6,2},{7,3},{8,4},{9,5},{10,6},{11,7},{12,8},{13,9},{1... | collective-permute-start | bytes 6152 | tf_op jit(solution)/shard_map/ppermute | solution.py:41
  30.3 3.7 %collective-permute-start.6 = (f32[1,512]{1,0:T(1,128)S(1)}, f32[1,512]{1,0:T(1,128)S(1)}, u32[]{:S(2)}, u32[]{:S(2)}) collective-permute-start(f32[1,512]{1,0:T(1,128)S(1)} %slice_maximum_fusion), channel_id=1, source_target_pairs={{0,2},{1,3},{2,0},{3,1},{4,6},{5,7},{6,4},{7,5},{8,10},{9,11},{10,... | collective-permute-start | bytes 6152 | tf_op jit(solution)/shard_map/ppermute | solution.py:19
where the time goes:
time: 34.4 us; the launch traced here: 34.6 us
  waiting for transfers between devices  20.2 us (59%)
  starting transfers between devices  8.88 us (26%)
  Pallas kernels  4.86 us (14%)
  other arithmetic  0.59 us (2%)
    ppermute x5, waiting for transfers between devices, swapped(): return lax.ppermute(array, 'shift', [(i, i ^ mask) for i in range(length)])  19.2 us
    ppermute x5, starting transfers between devices, swapped(): return lax.ppermute(array, 'shift', [(i, i ^ mask) for i in range(length)])  4.95 us
    pallas_call x5, Pallas kernels, call(): pl.pallas_call(kernel, out_shape=outs, in_specs=specs + [vmem] * (len(inp...  4.86 us
    ppermute x1, starting transfers between devices, backward(): lax.ppermute(array, ('parts', 'shift'), [(b, a) for a, b in next_quad()])  2.35 us
    ppermute x1, starting transfers between devices, forward(): return lax.ppermute(array, ('parts', 'shift'), next_quad())  1.58 us
    ppermute x1, waiting for transfers between devices, forward(): return lax.ppermute(array, ('parts', 'shift'), next_quad())  0.74 us
  transfers between devices with their start and end apart: 7, of which 5 were waited for; matrix products, arithmetic and copies ran while one was open for 0% of the time, Pallas kernels for 6%

commit v1 on v0

--- a/solution.py
+++ b/solution.py
@@ -33,6 +33,13 @@
     return pairs
 
 
+def ends():
+    count, mine = lax.axis_size("shift"), lax.axis_index("shift")
+    low, high = mine >= QUAD, mine + QUAD < count
+    upward = lax.axis_index("parts") % 2 == 0
+    return jnp.where(upward, low, high), jnp.where(upward, high, low)
+
+
 def forward(array):
     return lax.ppermute(array, ("parts", "shift"), next_quad())
 
@@ -55,11 +62,11 @@
     )
 
 
-def ids_of(packet, valid=None):
+def ids_of(packet, behind=False):
     blocks = packet.shape[0] - PAD
     values = packet[blocks:, :LANES].astype(jnp.float32)
-    if valid is not None:
-        values = jnp.where(valid[0] != 0, values, -1.0)
+    if behind:
+        values = jnp.where(ends()[0], values, -1.0)
     count = blocks // BLOCK
     return [jnp.broadcast_to(values[b : b + 1], (8, LANES)) for b in range(count)]
 
@@ -147,70 +154,45 @@
         best[...] = jnp.maximum(best[...], column_best(partner, own, sims))
 
 
-def first_kernel(
-    valid, own_ref, mate_ref, cross_ref, back_ref, best_in, best, to_mate, back
+def behind_kernel(
+    own_ref, mate_ref, partner_ref, behind_ref, best_in, best, to_mate, to_partner, back
 ):
-    own, mate, cross = ids_of(own_ref), ids_of(mate_ref), ids_of(cross_ref)
-    behind = ids_of(back_ref, valid)
+    own, mate, partner = ids_of(own_ref), ids_of(mate_ref), ids_of(partner_ref)
+    behind = ids_of(behind_ref, behind=True)
     best[...] = best_in[...]
-    back[...] = jnp.full_like(back, LOW)
-    to_mate[...] = jnp.full_like(to_mate, LOW)
-    hits = [shares(mate, behind), shares(cross, behind), shares(cross, own)]
-
-    for row, (ids, held) in enumerate(((mate, mate_ref), (cross, cross_ref))):
-
-        @pl.when(hits[row])
-        def _(row=row, ids=ids, held=held):
-            sims = product(rows_of(held), rows_of(back_ref))
+    for out in (to_mate, to_partner, back):
+        out[...] = jnp.full_like(out, LOW)
+    pairs = ((mate, mate_ref, to_mate), (own, own_ref, best), (partner, partner_ref, to_partner))
+    hits = [shares(ids, behind) for ids, held, out in pairs]
+    for hit, (ids, held, out) in zip(hits, pairs):
+
+        @pl.when(hit)
+        def _(ids=ids, held=held, out=out):
+            sims = product(rows_of(held), rows_of(behind_ref))
             back[...] = jnp.maximum(back[...], column_best(ids, behind, sims))
-            to_mate[row : row + 1, :] = row_best(ids, behind, sims)
-
-    @pl.when(hits[2])
+            out[...] = jnp.maximum(out[...], row_best(ids, behind, sims))
+
+
+def cross_kernel(cross_ref, behind_ref, to_mate_in, back_in, to_mate, back):
+    cross, behind = ids_of(cross_ref), ids_of(behind_ref, behind=True)
+    to_mate[0:1, :] = to_mate_in[...]
+    to_mate[1:2, :] = jnp.full_like(to_mate_in, LOW)
+    back[...] = back_in[...]
+
+    @pl.when(shares(cross, behind))
     def _():
-        sims = product(rows_of(cross_ref), rows_of(own_ref))
-        best[...] = jnp.maximum(best[...], column_best(cross, own, sims))
-
-
-def second_kernel(
-    valid, own_ref, partner_ref, back_ref, best_in, back_in, best, to_partner, back
-):
-    own, partner = ids_of(own_ref), ids_of(partner_ref)
-    behind = ids_of(back_ref, valid)
-    best[...] = best_in[...]
-    back[...] = back_in[...]
-    to_partner[...] = jnp.full_like(to_partner, LOW)
-    hits = [shares(own, behind), shares(partner, behind)]
-
-    @pl.when(hits[0])
-    def _():
-        sims = product(rows_of(own_ref), rows_of(back_ref))
-        back[...] = jnp.maximum(back[...], column_best(own, behind, sims))
-        best[...] = jnp.maximum(best[...], row_best(own, behind, sims))
-
-    @pl.when(hits[1])
-    def _():
-        sims = product(rows_of(partner_ref), rows_of(back_ref))
-        back[...] = jnp.maximum(back[...], column_best(partner, behind, sims))
-        to_partner[...] = row_best(partner, behind, sims)
+        sims = product(rows_of(cross_ref), rows_of(behind_ref))
+        back[...] = jnp.maximum(back[...], column_best(cross, behind, sims))
+        to_mate[1:2, :] = row_best(cross, behind, sims)
 
 
 def local(embeddings, block_cluster):
     rows, depth = embeddings.shape
-    count = lax.axis_size("shift")
-    mine = lax.axis_index("shift")
-    upward = lax.axis_index("parts") % 2 == 0
-    has_quad_below = mine >= QUAD
-    has_quad_above = mine + QUAD < count
-    receives = jnp.where(upward, has_quad_below, has_quad_above)
-    returns = jnp.where(upward, has_quad_above, has_quad_below)
-    valid = receives.astype(jnp.int32).reshape(1)
-
-    smem = pl.BlockSpec(memory_space=pltpu.SMEM)
     vmem = pl.BlockSpec(memory_space=pltpu.VMEM)
     line = jax.ShapeDtypeStruct((1, rows), jnp.float32)
     lines = jax.ShapeDtypeStruct((2, rows), jnp.float32)
 
-    def call(kernel, products, outs, specs, inputs, scratch=(), limit=40):
+    def call(kernel, products, outs, specs, inputs, scratch=(), limit=16):
         return pl.pallas_call(
             kernel,
             out_shape=outs,
@@ -243,14 +225,15 @@
     partner, best = lax.optimization_barrier((partner, best))
     cross = swapped(partner, 1)
     (best,) = call(partner_kernel, 0, (line,), [], (packet, partner, best))
-    best, to_mate, back = call(
-        first_kernel, 3, (line, lines, line), [smem], (valid, packet, mate, cross, behind, best)
+    best, to_mate, to_partner, back = call(
+        behind_kernel, 3, (line,) * 4, [], (packet, mate, partner, behind, best)
+    )
+    to_mate, back = call(
+        cross_kernel, 1, (lines, line), [], (cross, behind, to_mate, back)
     )
     from_mate = swapped(to_mate, 1)
-    best, to_partner, back = call(
-        second_kernel, 2, (line, line, line), [smem], (valid, packet, partner, behind, best, back)
-    )
-    from_next = jnp.where(returns, backward(back), LOW)
+    (best,) = call(partner_kernel, 1, (line,), [], (packet, cross, best))
+    from_next = jnp.where(ends()[1], backward(back), LOW)
     from_partner = swapped(jnp.maximum(to_partner, from_mate[1:2]), 2)
     best = jnp.maximum(jnp.maximum(best, from_next), jnp.maximum(from_mate[0:1], from_partner))
     return jnp.maximum(best.reshape(rows), -1.0)

time: 34.4 us -> 32.9 us (0.956); the launches traced: 34.6 us -> 32.6 us
  Pallas kernels: 4.86 us -> 3.84 us
  starting transfers between devices: 8.88 us -> 8.22 us
    pallas_call x5 -> x6, Pallas kernels: 4.86 us -> 3.84 us  [call(): pl.pallas_call(kernel, out_shape=outs, in_specs=specs + [vmem] * (len(inp...]
    ppermute x5, starting transfers between devices: 4.95 us -> 4.22 us  [swapped(): return lax.ppermute(array, 'shift', [(i, i ^ mask) for i in range(length)])]
  transfers between devices with their start and end apart: 7 -> 7, of which waited for: 5 -> 5; matrix products, arithmetic and copies ran while one was open for 0% -> 0% of each run, Pallas kernels for 6% -> 7%
where the time goes in v1:
time: 32.9 us; the launch traced here: 32.6 us
  waiting for transfers between devices  19.9 us (60%)
  starting transfers between devices  8.22 us (25%)
  Pallas kernels  3.84 us (12%)
  other arithmetic  0.59 us (2%)
    ppermute x5, waiting for transfers between devices, swapped(): return lax.ppermute(array, 'shift', [(i, i ^ mask) for i in range(length)])  18.9 us
    ppermute x5, starting transfers between devices, swapped(): return lax.ppermute(array, 'shift', [(i, i ^ mask) for i in range(length)])  4.22 us
    pallas_call x6, Pallas kernels, call(): pl.pallas_call(kernel, out_shape=outs, in_specs=specs + [vmem] * (len(inp...  3.84 us
    ppermute x1, starting transfers between devices, backward(): lax.ppermute(array, ('parts', 'shift'), [(b, a) for a, b in next_quad()])  2.42 us
    ppermute x1, starting transfers between devices, forward(): return lax.ppermute(array, ('parts', 'shift'), next_quad())  1.58 us
    ppermute x1, waiting for transfers between devices, forward(): return lax.ppermute(array, ('parts', 'shift'), next_quad())  0.74 us
  transfers between devices with their start and end apart: 7, of which 5 were waited for; matrix products, arithmetic and copies ran while one was open for 0% of the time, Pallas kernels for 7%

profile of v1, /device:TPU:0, one launch (start us, length us, event | category | flops | bytes accessed | tf_op | source)
XLA Modules:
  0.0 32.6 jit_solution(9323963420093077779)
XLA Ops:
  0.0 1.5 %shard_map.28.own_ref = bf16[528,768]{1,0:T(8,128)(2,1)S(1)} custom-call(s32[4]{0:T(128)} %ids_hbm.1, bf16[512,768]{1,0:T(8,128)(2,1)} %own_hbm.1), custom_call_target="tpu_custom_call" | custom-call | bytes 786432 | tf_op jit(solution)/shard_map/pallas_call | solution.py:196
  1.5 0.5 %collective-permute-start.1 = (bf16[528,768]{1,0:T(8,128)(2,1)S(1)}, bf16[528,768]{1,0:T(8,128)(2,1)S(1)}, u32[]{:S(2)}, u32[]{:S(2)}) collective-permute-start(bf16[528,768]{1,0:T(8,128)(2,1)S(1)} %shard_map.28.own_ref), channel_id=1, source_target_pairs={{0,1},{1,0},{2,3},{3,2},{4,5},{5,4},{6,7},{7,6},{8,9},{9,8},{10,11... | collective-permute-start | bytes 2433032 | tf_op jit(solution)/shard_map/ppermute | solution.py:19
  2.0 2.6 %collective-permute-start = (bf16[528,768]{1,0:T(8,128)(2,1)S(1)}, bf16[528,768]{1,0:T(8,128)(2,1)S(1)}, u32[]{:S(2)}, u32[]{:S(2)}) collective-permute-start(bf16[528,768]{1,0:T(8,128)(2,1)S(1)} %shard_map.28.own_ref), channel_id=1, source_target_pairs={{0,2},{1,3},{2,0},{3,1},{4,6},{5,7},{6,4},{7,5},{8,10},{9,11},{10,... | collective-permute-start | bytes 2433032 | tf_op jit(solution)/shard_map/ppermute | solution.py:19
  4.6 1.6 %collective-permute-start.3 = (bf16[528,768]{1,0:T(8,128)(2,1)S(1)}, bf16[528,768]{1,0:T(8,128)(2,1)S(1)}, u32[]{:S(2)}, u32[]{:S(2)}) collective-permute-start(bf16[528,768]{1,0:T(8,128)(2,1)S(1)} %shard_map.28.own_ref), channel_id=1, source_target_pairs={{0,4},{1,5},{2,6},{3,7},{4,8},{5,9},{6,10},{7,11},{8,12},{9,13},{1... | collective-permute-start | bytes 2433032 | tf_op jit(solution)/shard_map/ppermute | solution.py:44
  6.2 0.0 collective-permute-done.1.mate_ref
  6.2 1.2 %shard_map.29.best_in = f32[1,512]{1,0:T(1,128)S(1)} custom-call(bf16[528,768]{1,0:T(8,128)(2,1)S(1)} %shard_map.28.own_ref, bf16[528,768]{1,0:T(8,128)(2,1)S(1)} %collective-permute-done.1.mate_ref), custom_call_target="tpu_custom_call" | custom-call | bytes 786432 | tf_op jit(solution)/shard_map/pallas_call | solution.py:196
  7.4 15.8 %collective-permute-done.partner_ref = bf16[528,768]{1,0:T(8,128)(2,1)S(1)} collective-permute-done((bf16[528,768]{1,0:T(8,128)(2,1)S(1)}, bf16[528,768]{1,0:T(8,128)(2,1)S(1)}, u32[]{:S(2)}, u32[]{:S(2)}) %collective-permute-start) | collective-permute-done | bytes 811040 | tf_op jit(solution)/shard_map/ppermute | solution.py:19
  23.3 0.0 collective-permute-start.2
  23.3 0.7 %shard_map.30.best_in = f32[1,512]{1,0:T(1,128)S(1)} custom-call(bf16[528,768]{1,0:T(8,128)(2,1)S(1)} %shard_map.28.own_ref, bf16[528,768]{1,0:T(8,128)(2,1)S(1)} %collective-permute-done.partner_ref, f32[1,512]{1,0:T(1,128)S(1)} %shard_map.29.best_in), custom_call_target="tpu_custom_call" | custom-call | bytes 786432 | tf_op jit(solution)/shard_map/pallas_call | solution.py:196
  24.0 0.7 %collective-permute-done.3.behind_ref = bf16[528,768]{1,0:T(8,128)(2,1)S(1)} collective-permute-done((bf16[528,768]{1,0:T(8,128)(2,1)S(1)}, bf16[528,768]{1,0:T(8,128)(2,1)S(1)}, u32[]{:S(2)}, u32[]{:S(2)}) %collective-permute-start.3) | collective-permute-done | bytes 811040 | tf_op jit(solution)/shard_map/ppermute | solution.py:44
  24.8 0.1 shard_map.31
  24.9 0.7 %collective-permute-done.2.partner_ref.cross_ref = bf16[528,768]{1,0:T(8,128)(2,1)S(1)} collective-permute-done((bf16[528,768]{1,0:T(8,128)(2,1)S(1)}, bf16[528,768]{1,0:T(8,128)(2,1)S(1)}, u32[]{:S(2)}, u32[]{:S(2)}) %collective-permute-start.2) | collective-permute-done | bytes 811040 | tf_op jit(solution)/shard_map/ppermute | solution.py:19
  25.6 0.1 shard_map.33
  25.7 0.2 collective-permute-start.5
  25.9 2.4 %collective-permute-start.4 = (f32[1,512]{1,0:T(1,128)S(1)}, f32[1,512]{1,0:T(1,128)S(1)}, u32[]{:S(2)}, u32[]{:S(2)}) collective-permute-start(f32[1,512]{1,0:T(1,128)S(1)} %get-tuple-element.18), channel_id=1, source_target_pairs={{4,0},{5,1},{6,2},{7,3},{8,4},{9,5},{10,6},{11,7},{12,8},{13,9},{1... | collective-permute-start | bytes 6152 | tf_op jit(solution)/shard_map/ppermute | solution.py:48
  28.4 0.0 collective-permute-done.5
  28.4 0.9 %collective-permute-start.6 = (f32[1,512]{1,0:T(1,128)S(1)}, f32[1,512]{1,0:T(1,128)S(1)}, u32[]{:S(2)}, u32[]{:S(2)}) collective-permute-start(f32[1,512]{1,0:T(1,128)S(1)} %slice_maximum_fusion), channel_id=1, source_target_pairs={{0,2},{1,3},{2,0},{3,1},{4,6},{5,7},{6,4},{7,5},{8,10},{9,11},{10,... | collective-permute-start | bytes 6152 | tf_op jit(solution)/shard_map/ppermute | solution.py:19
  29.3 0.1 shard_map.32
  29.4 0.3 collective-permute-done.4
  29.7 2.4 %collective-permute-done.6 = f32[1,512]{1,0:T(1,128)S(1)} collective-permute-done((f32[1,512]{1,0:T(1,128)S(1)}, f32[1,512]{1,0:T(1,128)S(1)}, u32[]{:S(2)}, u32[]{:S(2)}) %collective-permute-start.6) | collective-permute-done | bytes 2080 | tf_op jit(solution)/shard_map/ppermute | solution.py:19
  32.0 0.6 %fusion.2 = f32[1,512]{1,0:T(1,128)} fusion(f32[1,512]{1,0:T(1,128)S(1)} %collective-permute-done.6, f32[2,512]{1,0:T(2,128)S(1)} %collective-permute-done.5, f32[1,512]{1,0:T(1,128)S(1)} %shard_map.32, f32[1,512]{1,0:T(1,128)S(1)} %collective-permute-done.4, pred[]{:T(512)S(6)} %select_n.20), kind=kLoop, calls=%fused_computation.5 | loop fusion | flops 2560 | bytes 10241 | tf_op jit(solution)/shard_map/max | solution.py:239
  (1 shorter events, 0.0 us)
Async XLA Ops:
  1.5 4.7 %collective-permute-start.1 = (bf16[528,768]{1,0:T(8,128)(2,1)S(1)}, bf16[528,768]{1,0:T(8,128)(2,1)S(1)}, u32[]{:S(2)}, u32[]{:S(2)}) collective-permute-start(bf16[528,768]{1,0:T(8,128)(2,1)S(1)} %shard_map.28.own_ref), channel_id=1, source_target_pairs={{0,1},{1,0},{2,3},{3,2},{4,5},{5,4},{6,7},{7,6},{8,9},{9,8},{10,11... | collective-permute-start | bytes 2433032 | tf_op jit(solution)/shard_map/ppermute | solution.py:19
  2.0 21.3 %collective-permute-start = (bf16[528,768]{1,0:T(8,128)(2,1)S(1)}, bf16[528,768]{1,0:T(8,128)(2,1)S(1)}, u32[]{:S(2)}, u32[]{:S(2)}) collective-permute-start(bf16[528,768]{1,0:T(8,128)(2,1)S(1)} %shard_map.28.own_ref), channel_id=1, source_target_pairs={{0,2},{1,3},{2,0},{3,1},{4,6},{5,7},{6,4},{7,5},{8,10},{9,11},{10,... | collective-permute-start | bytes 2433032 | tf_op jit(solution)/shard_map/ppermute | solution.py:19
  4.6 20.1 %collective-permute-start.3 = (bf16[528,768]{1,0:T(8,128)(2,1)S(1)}, bf16[528,768]{1,0:T(8,128)(2,1)S(1)}, u32[]{:S(2)}, u32[]{:S(2)}) collective-permute-start(bf16[528,768]{1,0:T(8,128)(2,1)S(1)} %shard_map.28.own_ref), channel_id=1, source_target_pairs={{0,4},{1,5},{2,6},{3,7},{4,8},{5,9},{6,10},{7,11},{8,12},{9,13},{1... | collective-permute-start | bytes 2433032 | tf_op jit(solution)/shard_map/ppermute | solution.py:44
  23.3 2.3 %collective-permute-start.2 = (bf16[528,768]{1,0:T(8,128)(2,1)S(1)}, bf16[528,768]{1,0:T(8,128)(2,1)S(1)}, u32[]{:S(2)}, u32[]{:S(2)}) collective-permute-start(bf16[528,768]{1,0:T(8,128)(2,1)S(1)} %collective-permute-done.partner_ref), channel_id=1, source_target_pairs={{0,1},{1,0},{2,3},{3,2},{4,5},{5,4},{6,7},{7,6},{8,9},{9,8},{10,11... | collective-permute-start | bytes 2433032 | tf_op jit(solution)/shard_map/ppermute | solution.py:19
  25.7 2.6 %collective-permute-start.5 = (f32[2,512]{1,0:T(2,128)S(1)}, f32[2,512]{1,0:T(2,128)S(1)}, u32[]{:S(2)}, u32[]{:S(2)}) collective-permute-start(f32[2,512]{1,0:T(2,128)S(1)} %get-tuple-element.19), channel_id=1, source_target_pairs={{0,1},{1,0},{2,3},{3,2},{4,5},{5,4},{6,7},{7,6},{8,9},{9,8},{10,11... | collective-permute-start | bytes 12296 | tf_op jit(solution)/shard_map/ppermute | solution.py:19
  25.9 3.7 %collective-permute-start.4 = (f32[1,512]{1,0:T(1,128)S(1)}, f32[1,512]{1,0:T(1,128)S(1)}, u32[]{:S(2)}, u32[]{:S(2)}) collective-permute-start(f32[1,512]{1,0:T(1,128)S(1)} %get-tuple-element.18), channel_id=1, source_target_pairs={{4,0},{5,1},{6,2},{7,3},{8,4},{9,5},{10,6},{11,7},{12,8},{13,9},{1... | collective-permute-start | bytes 6152 | tf_op jit(solution)/shard_map/ppermute | solution.py:48
  28.4 3.7 %collective-permute-start.6 = (f32[1,512]{1,0:T(1,128)S(1)}, f32[1,512]{1,0:T(1,128)S(1)}, u32[]{:S(2)}, u32[]{:S(2)}) collective-permute-start(f32[1,512]{1,0:T(1,128)S(1)} %slice_maximum_fusion), channel_id=1, source_target_pairs={{0,2},{1,3},{2,0},{3,1},{4,6},{5,7},{6,4},{7,5},{8,10},{9,11},{10,... | collective-permute-start | bytes 6152 | tf_op jit(solution)/shard_map/ppermute | solution.py:19

commit v2 on v1

--- a/solution.py
+++ b/solution.py
@@ -1,3 +1,4 @@
+import functools
 import math
 
 import jax
@@ -134,24 +135,32 @@
     packet[rows:, :] = ids.astype(jnp.bfloat16)
 
 
-def near_kernel(own_ref, mate_ref, best):
-    own, mate = ids_of(own_ref), ids_of(mate_ref)
+def own_kernel(own_ref, best):
+    own = ids_of(own_ref)
     best[...] = column_best(own, own, product(rows_of(own_ref), rows_of(own_ref)), own=True)
 
-    @pl.when(shares(mate, own))
+
+def near_kernel(own_ref, *refs):
+    *others, best_in, best = refs
+    own = ids_of(own_ref)
+    best[...] = best_in[...]
+    ids = [ids_of(other) for other in others]
+    hits = [shares(other, own) for other in ids]
+
+    def add(other, held):
+        sims = product(rows_of(held), rows_of(own_ref))
+        best[...] = jnp.maximum(best[...], column_best(other, own, sims))
+
+    every = functools.reduce(jnp.logical_and, hits)
+
+    @pl.when(every)
     def _():
-        sims = product(rows_of(mate_ref), rows_of(own_ref))
-        best[...] = jnp.maximum(best[...], column_best(mate, own, sims))
-
-
-def partner_kernel(own_ref, partner_ref, best_in, best):
-    own, partner = ids_of(own_ref), ids_of(partner_ref)
-    best[...] = best_in[...]
-
-    @pl.when(shares(partner, own))
-    def _():
-        sims = product(rows_of(partner_ref), rows_of(own_ref))
-        best[...] = jnp.maximum(best[...], column_best(partner, own, sims))
+        for pair in zip(ids, others):
+            add(*pair)
+
+    if len(others) > 1:
+        for hit, pair in zip(hits, zip(ids, others)):
+            pl.when(hit & ~every)(functools.partial(add, *pair))
 
 
 def behind_kernel(
@@ -164,13 +173,21 @@
         out[...] = jnp.full_like(out, LOW)
     pairs = ((mate, mate_ref, to_mate), (own, own_ref, best), (partner, partner_ref, to_partner))
     hits = [shares(ids, behind) for ids, held, out in pairs]
-    for hit, (ids, held, out) in zip(hits, pairs):
-
-        @pl.when(hit)
-        def _(ids=ids, held=held, out=out):
-            sims = product(rows_of(held), rows_of(behind_ref))
-            back[...] = jnp.maximum(back[...], column_best(ids, behind, sims))
-            out[...] = jnp.maximum(out[...], row_best(ids, behind, sims))
+
+    def add(ids, held, out):
+        sims = product(rows_of(held), rows_of(behind_ref))
+        back[...] = jnp.maximum(back[...], column_best(ids, behind, sims))
+        out[...] = jnp.maximum(out[...], row_best(ids, behind, sims))
+
+    several = (hits[0] & hits[1]) | (hits[0] & hits[2]) | (hits[1] & hits[2])
+
+    @pl.when(several)
+    def _():
+        for pair in pairs:
+            add(*pair)
+
+    for hit, pair in zip(hits, pairs):
+        pl.when(hit & ~several)(functools.partial(add, *pair))
 
 
 def cross_kernel(cross_ref, behind_ref, to_mate_in, back_in, to_mate, back):
@@ -184,6 +201,10 @@
         sims = product(rows_of(cross_ref), rows_of(behind_ref))
         back[...] = jnp.maximum(back[...], column_best(cross, behind, sims))
         to_mate[1:2, :] = row_best(cross, behind, sims)
+
+
+def join_kernel(best_in, from_mate, from_partner, best):
+    best[...] = jnp.maximum(jnp.maximum(best_in[...], from_mate[0:1, :]), from_partner[...])
 
 
 def local(embeddings, block_cluster):
@@ -221,10 +242,10 @@
     partner = swapped(packet, 2)
     behind = forward(packet)
     mate = swapped(packet, 1)
-    (best,) = call(near_kernel, 0, (line,), [], (packet, mate))
+    (best,) = call(own_kernel, 0, (line,), [], (packet,))
     partner, best = lax.optimization_barrier((partner, best))
     cross = swapped(partner, 1)
-    (best,) = call(partner_kernel, 0, (line,), [], (packet, partner, best))
+    (best,) = call(near_kernel, 0, (line,), [], (packet, partner, mate, best))
     best, to_mate, to_partner, back = call(
         behind_kernel, 3, (line,) * 4, [], (packet, mate, partner, behind, best)
     )
@@ -232,10 +253,12 @@
         cross_kernel, 1, (lines, line), [], (cross, behind, to_mate, back)
     )
     from_mate = swapped(to_mate, 1)
-    (best,) = call(partner_kernel, 1, (line,), [], (packet, cross, best))
-    from_next = jnp.where(ends()[1], backward(back), LOW)
+    (best,) = call(near_kernel, 1, (line,), [], (packet, cross, best))
+    from_mate, back, best = lax.optimization_barrier((from_mate, back, best))
     from_partner = swapped(jnp.maximum(to_partner, from_mate[1:2]), 2)
-    best = jnp.maximum(jnp.maximum(best, from_next), jnp.maximum(from_mate[0:1], from_partner))
+    from_next = backward(back)
+    (best,) = call(join_kernel, 0, (line,), [], (best, from_mate, from_partner))
+    best = jnp.maximum(best, jnp.where(ends()[1], from_next, LOW))
     return jnp.maximum(best.reshape(rows), -1.0)
 
 

time: 32.9 us -> 32.4 us (0.985)
  waiting for transfers between devices: 19.9 us -> 20.7 us
  starting transfers between devices: 8.22 us -> 7.64 us
  Pallas kernels: 3.84 us -> 3.27 us
    ppermute x5, waiting for transfers between devices: 18.9 us -> 17.5 us  [swapped(): return lax.ppermute(array, 'shift', [(i, i ^ mask) for i in range(length)])]
    ppermute x1, waiting for transfers between devices: 0.26 us -> 1.48 us  [backward(): lax.ppermute(array, ('parts', 'shift'), [(b, a) for a, b in next_quad()])]
    ppermute x1, starting transfers between devices: 2.42 us -> 1.49 us  [backward(): lax.ppermute(array, ('parts', 'shift'), [(b, a) for a, b in next_quad()])]
    ppermute x1, waiting for transfers between devices: 0.74 us -> 1.66 us  [forward(): return lax.ppermute(array, ('parts', 'shift'), next_quad())]
    pallas_call x6 -> x7, Pallas kernels: 3.84 us -> 3.27 us  [call(): pl.pallas_call(kernel, out_shape=outs, in_specs=specs + [vmem] * (len(inp...]
    ppermute x5, starting transfers between devices: 4.22 us -> 4.57 us  [swapped(): return lax.ppermute(array, 'shift', [(i, i ^ mask) for i in range(length)])]
  transfers between devices with their start and end apart: 7 -> 7, of which waited for: 5 -> 5; matrix products, arithmetic and copies ran while one was open for 0% -> 0% of each run, Pallas kernels for 7% -> 5%
where the time goes in v2:
time: 32.4 us; the launch traced here: 32.2 us
  waiting for transfers between devices  20.7 us (64%)
  starting transfers between devices  7.64 us (24%)
  Pallas kernels  3.27 us (10%)
  other arithmetic  0.59 us (2%)
    ppermute x5, waiting for transfers between devices, swapped(): return lax.ppermute(array, 'shift', [(i, i ^ mask) for i in range(length)])  17.5 us
    ppermute x5, starting transfers between devices, swapped(): return lax.ppermute(array, 'shift', [(i, i ^ mask) for i in range(length)])  4.57 us
    pallas_call x7, Pallas kernels, call(): pl.pallas_call(kernel, out_shape=outs, in_specs=specs + [vmem] * (len(inp...  3.27 us
    ppermute x1, waiting for transfers between devices, forward(): return lax.ppermute(array, ('parts', 'shift'), next_quad())  1.66 us
    ppermute x1, starting transfers between devices, forward(): return lax.ppermute(array, ('parts', 'shift'), next_quad())  1.58 us
    ppermute x1, starting transfers between devices, backward(): lax.ppermute(array, ('parts', 'shift'), [(b, a) for a, b in next_quad()])  1.49 us
    ppermute x1, waiting for transfers between devices, backward(): lax.ppermute(array, ('parts', 'shift'), [(b, a) for a, b in next_quad()])  1.48 us
  transfers between devices with their start and end apart: 7, of which 5 were waited for; matrix products, arithmetic and copies ran while one was open for 0% of the time, Pallas kernels for 5%

profile of v2, /device:TPU:0, one launch (start us, length us, event | category | flops | bytes accessed | tf_op | source)
XLA Modules:
  0.0 32.2 jit_solution(2590617634257243151)
XLA Ops:
  0.0 1.5 %shard_map.28.own_ref = bf16[528,768]{1,0:T(8,128)(2,1)S(1)} custom-call(s32[4]{0:T(128)} %ids_hbm.1, bf16[512,768]{1,0:T(8,128)(2,1)} %own_hbm.1), custom_call_target="tpu_custom_call" | custom-call | bytes 786432 | tf_op jit(solution)/shard_map/pallas_call | solution.py:217
  1.5 3.0 %collective-permute-start = (bf16[528,768]{1,0:T(8,128)(2,1)S(1)}, bf16[528,768]{1,0:T(8,128)(2,1)S(1)}, u32[]{:S(2)}, u32[]{:S(2)}) collective-permute-start(bf16[528,768]{1,0:T(8,128)(2,1)S(1)} %shard_map.28.own_ref), channel_id=1, source_target_pairs={{0,2},{1,3},{2,0},{3,1},{4,6},{5,7},{6,4},{7,5},{8,10},{9,11},{10,... | collective-permute-start | bytes 2433032 | tf_op jit(solution)/shard_map/ppermute | solution.py:20
  4.5 0.0 collective-permute-start.3
  4.6 1.6 %collective-permute-start.2 = (bf16[528,768]{1,0:T(8,128)(2,1)S(1)}, bf16[528,768]{1,0:T(8,128)(2,1)S(1)}, u32[]{:S(2)}, u32[]{:S(2)}) collective-permute-start(bf16[528,768]{1,0:T(8,128)(2,1)S(1)} %shard_map.28.own_ref), channel_id=1, source_target_pairs={{0,4},{1,5},{2,6},{3,7},{4,8},{5,9},{6,10},{7,11},{8,12},{9,13},{1... | collective-permute-start | bytes 2433032 | tf_op jit(solution)/shard_map/ppermute | solution.py:45
  6.1 0.6 %shard_map.29.refs_2_ = f32[1,512]{1,0:T(1,128)S(1)} custom-call(bf16[528,768]{1,0:T(8,128)(2,1)S(1)} %shard_map.28.own_ref), custom_call_target="tpu_custom_call" | custom-call | bytes 786432 | tf_op jit(solution)/shard_map/pallas_call | solution.py:217
  6.7 15.9 %collective-permute-done.refs_0_.partner_ref = bf16[528,768]{1,0:T(8,128)(2,1)S(1)} collective-permute-done((bf16[528,768]{1,0:T(8,128)(2,1)S(1)}, bf16[528,768]{1,0:T(8,128)(2,1)S(1)}, u32[]{:S(2)}, u32[]{:S(2)}) %collective-permute-start) | collective-permute-done | bytes 811040 | tf_op jit(solution)/shard_map/ppermute | solution.py:20
  22.6 0.0 collective-permute-start.1
  22.6 0.0 collective-permute-done.3.refs_1_.mate_ref
  22.6 0.7 %shard_map.30.best_in = f32[1,512]{1,0:T(1,128)S(1)} custom-call(bf16[528,768]{1,0:T(8,128)(2,1)S(1)} %shard_map.28.own_ref, bf16[528,768]{1,0:T(8,128)(2,1)S(1)} %collective-permute-done.refs_0_.partner_ref, bf16[528,768]{1,0:T(8,128)(2,1)S(1)} %collective-permute-done.3.refs_1_.mate_ref, f32[1,512]{1,0:T(1,128)S(1)} %shard_map.29.refs_2_), custom_call_target="tpu_custom_call" | custom-call | bytes 786432 | tf_op jit(solution)/shard_map/pallas_call | solution.py:217
  23.4 1.7 %collective-permute-done.2.behind_ref = bf16[528,768]{1,0:T(8,128)(2,1)S(1)} collective-permute-done((bf16[528,768]{1,0:T(8,128)(2,1)S(1)}, bf16[528,768]{1,0:T(8,128)(2,1)S(1)}, u32[]{:S(2)}, u32[]{:S(2)}) %collective-permute-start.2) | collective-permute-done | bytes 811040 | tf_op jit(solution)/shard_map/ppermute | solution.py:45
  25.0 0.1 shard_map.31
  25.2 0.0 collective-permute-done.1.cross_ref.refs_0_
  25.2 0.1 shard_map.32
  25.3 0.1 collective-permute-start.4
  25.4 0.1 shard_map.33.best_in
  25.5 1.0 %collective-permute-done.4.from_mate = f32[2,512]{1,0:T(2,128)S(1)} collective-permute-done((f32[2,512]{1,0:T(2,128)S(1)}, f32[2,512]{1,0:T(2,128)S(1)}, u32[]{:S(2)}, u32[]{:S(2)}) %collective-permute-start.4) | collective-permute-done | bytes 4128 | tf_op jit(solution)/shard_map/ppermute | solution.py:20
  26.6 1.5 %collective-permute-start.5 = (f32[1,512]{1,0:T(1,128)S(1)}, f32[1,512]{1,0:T(1,128)S(1)}, u32[]{:S(2)}, u32[]{:S(2)}) collective-permute-start(f32[1,512]{1,0:T(1,128)S(1)} %slice_maximum_fusion), channel_id=1, source_target_pairs={{0,2},{1,3},{2,0},{3,1},{4,6},{5,7},{6,4},{7,5},{8,10},{9,11},{10,... | collective-permute-start | bytes 6152 | tf_op jit(solution)/shard_map/ppermute | solution.py:20
  28.0 1.5 %collective-permute-start.6 = (f32[1,512]{1,0:T(1,128)S(1)}, f32[1,512]{1,0:T(1,128)S(1)}, u32[]{:S(2)}, u32[]{:S(2)}) collective-permute-start(f32[1,512]{1,0:T(1,128)S(1)} %get-tuple-element.26), channel_id=1, source_target_pairs={{4,0},{5,1},{6,2},{7,3},{8,4},{9,5},{10,6},{11,7},{12,8},{13,9},{1... | collective-permute-start | bytes 6152 | tf_op jit(solution)/shard_map/ppermute | solution.py:49
  29.5 0.6 %collective-permute-done.5.from_partner = f32[1,512]{1,0:T(1,128)S(1)} collective-permute-done((f32[1,512]{1,0:T(1,128)S(1)}, f32[1,512]{1,0:T(1,128)S(1)}, u32[]{:S(2)}, u32[]{:S(2)}) %collective-permute-start.5) | collective-permute-done | bytes 2080 | tf_op jit(solution)/shard_map/ppermute | solution.py:20
  30.2 1.5 %collective-permute-done.6 = f32[1,512]{1,0:T(1,128)S(1)} collective-permute-done((f32[1,512]{1,0:T(1,128)S(1)}, f32[1,512]{1,0:T(1,128)S(1)}, u32[]{:S(2)}, u32[]{:S(2)}) %collective-permute-start.6) | collective-permute-done | bytes 2080 | tf_op jit(solution)/shard_map/ppermute | solution.py:49
  31.7 0.6 %fusion.1 = f32[1,512]{1,0:T(1,128)} fusion(f32[1,512]{1,0:T(1,128)S(1)} %shard_map.34, f32[1,512]{1,0:T(1,128)S(1)} %collective-permute-done.6, pred[]{:T(512)S(6)} %select_n.20), kind=kLoop, calls=%fused_computation.2 | loop fusion | flops 1536 | bytes 6145 | tf_op jit(solution)/shard_map/max | solution.py:262
  (2 shorter events, 0.0 us)
Async XLA Ops:
  1.5 21.1 %collective-permute-start = (bf16[528,768]{1,0:T(8,128)(2,1)S(1)}, bf16[528,768]{1,0:T(8,128)(2,1)S(1)}, u32[]{:S(2)}, u32[]{:S(2)}) collective-permute-start(bf16[528,768]{1,0:T(8,128)(2,1)S(1)} %shard_map.28.own_ref), channel_id=1, source_target_pairs={{0,2},{1,3},{2,0},{3,1},{4,6},{5,7},{6,4},{7,5},{8,10},{9,11},{10,... | collective-permute-start | bytes 2433032 | tf_op jit(solution)/shard_map/ppermute | solution.py:20
  4.5 18.1 %collective-permute-start.3 = (bf16[528,768]{1,0:T(8,128)(2,1)S(1)}, bf16[528,768]{1,0:T(8,128)(2,1)S(1)}, u32[]{:S(2)}, u32[]{:S(2)}) collective-permute-start(bf16[528,768]{1,0:T(8,128)(2,1)S(1)} %shard_map.28.own_ref), channel_id=1, source_target_pairs={{0,1},{1,0},{2,3},{3,2},{4,5},{5,4},{6,7},{7,6},{8,9},{9,8},{10,11... | collective-permute-start | bytes 2433032 | tf_op jit(solution)/shard_map/ppermute | solution.py:20
  4.6 20.5 %collective-permute-start.2 = (bf16[528,768]{1,0:T(8,128)(2,1)S(1)}, bf16[528,768]{1,0:T(8,128)(2,1)S(1)}, u32[]{:S(2)}, u32[]{:S(2)}) collective-permute-start(bf16[528,768]{1,0:T(8,128)(2,1)S(1)} %shard_map.28.own_ref), channel_id=1, source_target_pairs={{0,4},{1,5},{2,6},{3,7},{4,8},{5,9},{6,10},{7,11},{8,12},{9,13},{1... | collective-permute-start | bytes 2433032 | tf_op jit(solution)/shard_map/ppermute | solution.py:45
  22.6 2.6 %collective-permute-start.1 = (bf16[528,768]{1,0:T(8,128)(2,1)S(1)}, bf16[528,768]{1,0:T(8,128)(2,1)S(1)}, u32[]{:S(2)}, u32[]{:S(2)}) collective-permute-start(bf16[528,768]{1,0:T(8,128)(2,1)S(1)} %collective-permute-done.refs_0_.partner_ref), channel_id=1, source_target_pairs={{0,1},{1,0},{2,3},{3,2},{4,5},{5,4},{6,7},{7,6},{8,9},{9,8},{10,11... | collective-permute-start | bytes 2433032 | tf_op jit(solution)/shard_map/ppermute | solution.py:20
  25.3 1.2 %collective-permute-start.4 = (f32[2,512]{1,0:T(2,128)S(1)}, f32[2,512]{1,0:T(2,128)S(1)}, u32[]{:S(2)}, u32[]{:S(2)}) collective-permute-start(f32[2,512]{1,0:T(2,128)S(1)} %get-tuple-element.20), channel_id=1, source_target_pairs={{0,1},{1,0},{2,3},{3,2},{4,5},{5,4},{6,7},{7,6},{8,9},{9,8},{10,11... | collective-permute-start | bytes 12296 | tf_op jit(solution)/shard_map/ppermute | solution.py:20
  26.6 3.6 %collective-permute-start.5 = (f32[1,512]{1,0:T(1,128)S(1)}, f32[1,512]{1,0:T(1,128)S(1)}, u32[]{:S(2)}, u32[]{:S(2)}) collective-permute-start(f32[1,512]{1,0:T(1,128)S(1)} %slice_maximum_fusion), channel_id=1, source_target_pairs={{0,2},{1,3},{2,0},{3,1},{4,6},{5,7},{6,4},{7,5},{8,10},{9,11},{10,... | collective-permute-start | bytes 6152 | tf_op jit(solution)/shard_map/ppermute | solution.py:20
  28.0 3.6 %collective-permute-start.6 = (f32[1,512]{1,0:T(1,128)S(1)}, f32[1,512]{1,0:T(1,128)S(1)}, u32[]{:S(2)}, u32[]{:S(2)}) collective-permute-start(f32[1,512]{1,0:T(1,128)S(1)} %get-tuple-element.26), channel_id=1, source_target_pairs={{4,0},{5,1},{6,2},{7,3},{8,4},{9,5},{10,6},{11,7},{12,8},{13,9},{1... | collective-permute-start | bytes 6152 | tf_op jit(solution)/shard_map/ppermute | solution.py:49

commit v3 on v2

--- a/solution.py
+++ b/solution.py
@@ -13,6 +13,7 @@
 BLOCK = 128
 LANES = 128
 PAD = 16
+STEP = 256
 
 
 def swapped(array, mask):
@@ -116,16 +117,18 @@
 def packet_kernel(ids_hbm, own_hbm, packet, held, own_ids, sems, ids_sem):
     rows, depth = held.shape
     count = rows // BLOCK
+    step = STEP
+    pieces = rows // step
     copies = []
     ids_copy = pltpu.make_async_copy(ids_hbm, own_ids, ids_sem)
     ids_copy.start()
-    for b in range(count):
-        part = pl.ds(b * BLOCK, BLOCK)
+    for b in range(pieces):
+        part = pl.ds(b * step, step)
         copies.append(pltpu.make_async_copy(own_hbm.at[part], held.at[part], sems.at[b]))
         copies[b].start()
-    for b in range(count):
+    for b in range(pieces):
         copies[b].wait()
-        part = pl.ds(b * BLOCK, BLOCK)
+        part = pl.ds(b * step, step)
         packet[part, :] = unit_rows(held[part, :])
     ids_copy.wait()
     row = lax.broadcasted_iota(jnp.int32, (PAD, depth), 0)
@@ -190,28 +193,27 @@
         pl.when(hit & ~several)(functools.partial(add, *pair))
 
 
-def cross_kernel(cross_ref, behind_ref, to_mate_in, back_in, to_mate, back):
+def cross_kernel(cross_ref, behind_ref, back_in, to_cross, back):
     cross, behind = ids_of(cross_ref), ids_of(behind_ref, behind=True)
-    to_mate[0:1, :] = to_mate_in[...]
-    to_mate[1:2, :] = jnp.full_like(to_mate_in, LOW)
+    to_cross[...] = jnp.full_like(to_cross, LOW)
     back[...] = back_in[...]
 
     @pl.when(shares(cross, behind))
     def _():
         sims = product(rows_of(cross_ref), rows_of(behind_ref))
         back[...] = jnp.maximum(back[...], column_best(cross, behind, sims))
-        to_mate[1:2, :] = row_best(cross, behind, sims)
-
-
-def join_kernel(best_in, from_mate, from_partner, best):
-    best[...] = jnp.maximum(jnp.maximum(best_in[...], from_mate[0:1, :]), from_partner[...])
+        to_cross[...] = row_best(cross, behind, sims)
+
+
+def join_kernel(*refs):
+    *lines, best = refs
+    best[...] = jnp.maximum(functools.reduce(jnp.maximum, [line[...] for line in lines]), -1.0)
 
 
 def local(embeddings, block_cluster):
     rows, depth = embeddings.shape
     vmem = pl.BlockSpec(memory_space=pltpu.VMEM)
     line = jax.ShapeDtypeStruct((1, rows), jnp.float32)
-    lines = jax.ShapeDtypeStruct((2, rows), jnp.float32)
 
     def call(kernel, products, outs, specs, inputs, scratch=(), limit=16):
         return pl.pallas_call(
@@ -235,7 +237,7 @@
         (
             pltpu.VMEM((rows, depth), jnp.bfloat16),
             pltpu.SMEM(block_cluster.shape, jnp.int32),
-            pltpu.SemaphoreType.DMA((rows // BLOCK,)),
+            pltpu.SemaphoreType.DMA((rows // STEP,)),
             pltpu.SemaphoreType.DMA,
         ),
     )
@@ -249,17 +251,14 @@
     best, to_mate, to_partner, back = call(
         behind_kernel, 3, (line,) * 4, [], (packet, mate, partner, behind, best)
     )
-    to_mate, back = call(
-        cross_kernel, 1, (lines, line), [], (cross, behind, to_mate, back)
-    )
-    from_mate = swapped(to_mate, 1)
+    to_cross, back = call(cross_kernel, 1, (line, line), [], (cross, behind, back))
+    from_next = backward(back)
+    if lax.axis_size("parts") % 2:
+        from_next = jnp.where(ends()[1], from_next, LOW)
+    returned = (swapped(to_cross, 3), swapped(to_partner, 2), swapped(to_mate, 1), from_next)
     (best,) = call(near_kernel, 1, (line,), [], (packet, cross, best))
-    from_mate, back, best = lax.optimization_barrier((from_mate, back, best))
-    from_partner = swapped(jnp.maximum(to_partner, from_mate[1:2]), 2)
-    from_next = backward(back)
-    (best,) = call(join_kernel, 0, (line,), [], (best, from_mate, from_partner))
-    best = jnp.maximum(best, jnp.where(ends()[1], from_next, LOW))
-    return jnp.maximum(best.reshape(rows), -1.0)
+    (best,) = call(join_kernel, 0, (line,), [], (best, *returned))
+    return best.reshape(rows)
 
 
 def solution(mesh):

time: 32.4 us -> 31.8 us (0.981)
  waiting for transfers between devices: 20.7 us -> 19.1 us
  Pallas kernels: 3.27 us -> 4.11 us
  starting transfers between devices: 7.64 us -> 8.37 us
  other arithmetic: 0.59 us -> 0 us
    ppermute x5 -> x6, waiting for transfers between devices: 17.5 us -> 15.9 us  [swapped(): return lax.ppermute(array, 'shift', [(i, i ^ mask) for i in range(length)])]
    pallas_call x7, Pallas kernels: 3.27 us -> 4.11 us  [call(): pl.pallas_call(kernel, out_shape=outs, in_specs=specs + [vmem] * (len(inp...]
    ppermute x5 -> x6, starting transfers between devices: 4.57 us -> 5.3 us  [swapped(): return lax.ppermute(array, 'shift', [(i, i ^ mask) for i in range(length)])]
    max x2 -> x0, other arithmetic: 0.59 us -> none  [the longest x1 0.58 us: local(): return jnp.maximum(best.reshape(rows), -1.0)]
    ppermute x1, waiting for transfers between devices: 1.48 us -> 1.93 us  [backward(): lax.ppermute(array, ('parts', 'shift'), [(b, a) for a, b in next_quad()])]
    ppermute x1, waiting for transfers between devices: 1.66 us -> 1.25 us  [forward(): return lax.ppermute(array, ('parts', 'shift'), next_quad())]
  transfers between devices with their start and end apart: 7 -> 8, of which waited for: 5 -> 3; matrix products, arithmetic and copies ran while one was open for 0% -> 0% of each run, Pallas kernels for 5% -> 7%
where the time goes in v3:
time: 31.8 us; the launch traced here: 31.6 us
  waiting for transfers between devices  19.1 us (60%)
  starting transfers between devices  8.37 us (26%)
  Pallas kernels  4.11 us (13%)
    ppermute x6, waiting for transfers between devices, swapped(): return lax.ppermute(array, 'shift', [(i, i ^ mask) for i in range(length)])  15.9 us
    ppermute x6, starting transfers between devices, swapped(): return lax.ppermute(array, 'shift', [(i, i ^ mask) for i in range(length)])  5.3 us
    pallas_call x7, Pallas kernels, call(): pl.pallas_call(kernel, out_shape=outs, in_specs=specs + [vmem] * (len(inp...  4.11 us
    ppermute x1, waiting for transfers between devices, backward(): lax.ppermute(array, ('parts', 'shift'), [(b, a) for a, b in next_quad()])  1.93 us
    ppermute x1, starting transfers between devices, forward(): return lax.ppermute(array, ('parts', 'shift'), next_quad())  1.58 us
    ppermute x1, starting transfers between devices, backward(): lax.ppermute(array, ('parts', 'shift'), [(b, a) for a, b in next_quad()])  1.49 us
    ppermute x1, waiting for transfers between devices, forward(): return lax.ppermute(array, ('parts', 'shift'), next_quad())  1.25 us
  transfers between devices with their start and end apart: 8, of which 3 were waited for; matrix products, arithmetic and copies ran while one was open for 0% of the time, Pallas kernels for 7%

profile of v3, /device:TPU:0, one launch (start us, length us, event | category | flops | bytes accessed | tf_op | source)
XLA Modules:
  0.0 31.6 jit_solution(9541098580386836648)
XLA Ops:
  0.0 1.4 %shard_map.28.own_ref = bf16[528,768]{1,0:T(8,128)(2,1)S(1)} custom-call(s32[4]{0:T(128)} %ids_hbm.1, bf16[512,768]{1,0:T(8,128)(2,1)} %own_hbm.1), custom_call_target="tpu_custom_call" | custom-call | bytes 786432 | tf_op jit(solution)/shard_map/pallas_call | solution.py:219
  1.4 3.0 %collective-permute-start = (bf16[528,768]{1,0:T(8,128)(2,1)S(1)}, bf16[528,768]{1,0:T(8,128)(2,1)S(1)}, u32[]{:S(2)}, u32[]{:S(2)}) collective-permute-start(bf16[528,768]{1,0:T(8,128)(2,1)S(1)} %shard_map.28.own_ref), channel_id=1, source_target_pairs={{0,2},{1,3},{2,0},{3,1},{4,6},{5,7},{6,4},{7,5},{8,10},{9,11},{10,... | collective-permute-start | bytes 2433032 | tf_op jit(solution)/shard_map/ppermute | solution.py:21
  4.4 0.0 collective-permute-start.2
  4.4 1.6 %collective-permute-start.3 = (bf16[528,768]{1,0:T(8,128)(2,1)S(1)}, bf16[528,768]{1,0:T(8,128)(2,1)S(1)}, u32[]{:S(2)}, u32[]{:S(2)}) collective-permute-start(bf16[528,768]{1,0:T(8,128)(2,1)S(1)} %shard_map.28.own_ref), channel_id=1, source_target_pairs={{0,4},{1,5},{2,6},{3,7},{4,8},{5,9},{6,10},{7,11},{8,12},{9,13},{1... | collective-permute-start | bytes 2433032 | tf_op jit(solution)/shard_map/ppermute | solution.py:46
  6.0 0.6 %shard_map.29.refs_2_ = f32[1,512]{1,0:T(1,128)S(1)} custom-call(bf16[528,768]{1,0:T(8,128)(2,1)S(1)} %shard_map.28.own_ref), custom_call_target="tpu_custom_call" | custom-call | bytes 786432 | tf_op jit(solution)/shard_map/pallas_call | solution.py:219
  6.6 15.9 %collective-permute-done.refs_0_.partner_ref = bf16[528,768]{1,0:T(8,128)(2,1)S(1)} collective-permute-done((bf16[528,768]{1,0:T(8,128)(2,1)S(1)}, bf16[528,768]{1,0:T(8,128)(2,1)S(1)}, u32[]{:S(2)}, u32[]{:S(2)}) %collective-permute-start) | collective-permute-done | bytes 811040 | tf_op jit(solution)/shard_map/ppermute | solution.py:21
  22.5 0.0 collective-permute-start.1
  22.5 0.0 collective-permute-done.2.refs_1_.mate_ref
  22.5 1.2 %shard_map.30.best_in = f32[1,512]{1,0:T(1,128)S(1)} custom-call(bf16[528,768]{1,0:T(8,128)(2,1)S(1)} %shard_map.28.own_ref, bf16[528,768]{1,0:T(8,128)(2,1)S(1)} %collective-permute-done.refs_0_.partner_ref, bf16[528,768]{1,0:T(8,128)(2,1)S(1)} %collective-permute-done.2.refs_1_.mate_ref, f32[1,512]{1,0:T(1,128)S(1)} %shard_map.29.refs_2_), custom_call_target="tpu_custom_call" | custom-call | bytes 786432 | tf_op jit(solution)/shard_map/pallas_call | solution.py:219
  23.6 1.2 %collective-permute-done.3.behind_ref = bf16[528,768]{1,0:T(8,128)(2,1)S(1)} collective-permute-done((bf16[528,768]{1,0:T(8,128)(2,1)S(1)}, bf16[528,768]{1,0:T(8,128)(2,1)S(1)}, u32[]{:S(2)}, u32[]{:S(2)}) %collective-permute-start.3) | collective-permute-done | bytes 811040 | tf_op jit(solution)/shard_map/ppermute | solution.py:46
  24.9 0.1 shard_map.31
  25.0 0.6 %collective-permute-start.5 = (f32[1,512]{1,0:T(1,128)S(1)}, f32[1,512]{1,0:T(1,128)S(1)}, u32[]{:S(2)}, u32[]{:S(2)}) collective-permute-start(f32[1,512]{1,0:T(1,128)S(1)} %get-tuple-element.18), channel_id=1, source_target_pairs={{0,2},{1,3},{2,0},{3,1},{4,6},{5,7},{6,4},{7,5},{8,10},{9,11},{10,... | collective-permute-start | bytes 6152 | tf_op jit(solution)/shard_map/ppermute | solution.py:21
  25.6 0.0 collective-permute-start.6
  25.6 0.0 collective-permute-done.1.refs_0_.cross_ref
  25.6 0.1 shard_map.33
  25.8 1.7 %collective-permute-start.4 = (f32[1,512]{1,0:T(1,128)S(1)}, f32[1,512]{1,0:T(1,128)S(1)}, u32[]{:S(2)}, u32[]{:S(2)}) collective-permute-start(f32[1,512]{1,0:T(1,128)S(1)} %get-tuple-element.17), channel_id=1, source_target_pairs={{0,3},{1,2},{2,1},{3,0},{4,7},{5,6},{6,5},{7,4},{8,11},{9,10},{10,... | collective-permute-start | bytes 6152 | tf_op jit(solution)/shard_map/ppermute | solution.py:21
  27.4 1.5 %collective-permute-start.7 = (f32[1,512]{1,0:T(1,128)S(1)}, f32[1,512]{1,0:T(1,128)S(1)}, u32[]{:S(2)}, u32[]{:S(2)}) collective-permute-start(f32[1,512]{1,0:T(1,128)S(1)} %get-tuple-element.20), channel_id=1, source_target_pairs={{4,0},{5,1},{6,2},{7,3},{8,4},{9,5},{10,6},{11,7},{12,8},{13,9},{1... | collective-permute-start | bytes 6152 | tf_op jit(solution)/shard_map/ppermute | solution.py:50
  28.9 0.1 shard_map.32.refs_0_
  29.1 0.0 collective-permute-done.5.refs_2_
  29.1 0.0 collective-permute-done.6.refs_3_
  29.1 0.0 collective-permute-done.4.refs_1_
  29.1 1.9 %collective-permute-done.7.refs_4_ = f32[1,512]{1,0:T(1,128)S(1)} collective-permute-done((f32[1,512]{1,0:T(1,128)S(1)}, f32[1,512]{1,0:T(1,128)S(1)}, u32[]{:S(2)}, u32[]{:S(2)}) %collective-permute-start.7) | collective-permute-done | bytes 2080 | tf_op jit(solution)/shard_map/ppermute | solution.py:50
  31.0 0.6 %shard_map.34 = f32[1,512]{1,0:T(1,128)} custom-call(f32[1,512]{1,0:T(1,128)S(1)} %shard_map.32.refs_0_, f32[1,512]{1,0:T(1,128)S(1)} %collective-permute-done.4.refs_1_, f32[1,512]{1,0:T(1,128)S(1)} %collective-permute-done.5.refs_2_, f32[1,512]{1,0:T(1,128)S(1)} %collective-permute-done.6.refs_3_, f32[1,512]{1,0:T(1,128)S(1)} %collective-permute-done.7.refs_4_), custom_call_target="tpu_custom_call" | custom-call | bytes 786432 | tf_op jit(solution)/shard_map/pallas_call | solution.py:219
Async XLA Ops:
  1.4 21.1 %collective-permute-start = (bf16[528,768]{1,0:T(8,128)(2,1)S(1)}, bf16[528,768]{1,0:T(8,128)(2,1)S(1)}, u32[]{:S(2)}, u32[]{:S(2)}) collective-permute-start(bf16[528,768]{1,0:T(8,128)(2,1)S(1)} %shard_map.28.own_ref), channel_id=1, source_target_pairs={{0,2},{1,3},{2,0},{3,1},{4,6},{5,7},{6,4},{7,5},{8,10},{9,11},{10,... | collective-permute-start | bytes 2433032 | tf_op jit(solution)/shard_map/ppermute | solution.py:21
  4.4 18.1 %collective-permute-start.2 = (bf16[528,768]{1,0:T(8,128)(2,1)S(1)}, bf16[528,768]{1,0:T(8,128)(2,1)S(1)}, u32[]{:S(2)}, u32[]{:S(2)}) collective-permute-start(bf16[528,768]{1,0:T(8,128)(2,1)S(1)} %shard_map.28.own_ref), channel_id=1, source_target_pairs={{0,1},{1,0},{2,3},{3,2},{4,5},{5,4},{6,7},{7,6},{8,9},{9,8},{10,11... | collective-permute-start | bytes 2433032 | tf_op jit(solution)/shard_map/ppermute | solution.py:21
  4.4 20.5 %collective-permute-start.3 = (bf16[528,768]{1,0:T(8,128)(2,1)S(1)}, bf16[528,768]{1,0:T(8,128)(2,1)S(1)}, u32[]{:S(2)}, u32[]{:S(2)}) collective-permute-start(bf16[528,768]{1,0:T(8,128)(2,1)S(1)} %shard_map.28.own_ref), channel_id=1, source_target_pairs={{0,4},{1,5},{2,6},{3,7},{4,8},{5,9},{6,10},{7,11},{8,12},{9,13},{1... | collective-permute-start | bytes 2433032 | tf_op jit(solution)/shard_map/ppermute | solution.py:46
  22.5 3.2 %collective-permute-start.1 = (bf16[528,768]{1,0:T(8,128)(2,1)S(1)}, bf16[528,768]{1,0:T(8,128)(2,1)S(1)}, u32[]{:S(2)}, u32[]{:S(2)}) collective-permute-start(bf16[528,768]{1,0:T(8,128)(2,1)S(1)} %collective-permute-done.refs_0_.partner_ref), channel_id=1, source_target_pairs={{0,1},{1,0},{2,3},{3,2},{4,5},{5,4},{6,7},{7,6},{8,9},{9,8},{10,11... | collective-permute-start | bytes 2433032 | tf_op jit(solution)/shard_map/ppermute | solution.py:21
  25.0 4.0 %collective-permute-start.5 = (f32[1,512]{1,0:T(1,128)S(1)}, f32[1,512]{1,0:T(1,128)S(1)}, u32[]{:S(2)}, u32[]{:S(2)}) collective-permute-start(f32[1,512]{1,0:T(1,128)S(1)} %get-tuple-element.18), channel_id=1, source_target_pairs={{0,2},{1,3},{2,0},{3,1},{4,6},{5,7},{6,4},{7,5},{8,10},{9,11},{10,... | collective-permute-start | bytes 6152 | tf_op jit(solution)/shard_map/ppermute | solution.py:21
  25.6 3.5 %collective-permute-start.6 = (f32[1,512]{1,0:T(1,128)S(1)}, f32[1,512]{1,0:T(1,128)S(1)}, u32[]{:S(2)}, u32[]{:S(2)}) collective-permute-start(f32[1,512]{1,0:T(1,128)S(1)} %get-tuple-element.19), channel_id=1, source_target_pairs={{0,1},{1,0},{2,3},{3,2},{4,5},{5,4},{6,7},{7,6},{8,9},{9,8},{10,11... | collective-permute-start | bytes 6152 | tf_op jit(solution)/shard_map/ppermute | solution.py:21
  25.8 3.3 %collective-permute-start.4 = (f32[1,512]{1,0:T(1,128)S(1)}, f32[1,512]{1,0:T(1,128)S(1)}, u32[]{:S(2)}, u32[]{:S(2)}) collective-permute-start(f32[1,512]{1,0:T(1,128)S(1)} %get-tuple-element.17), channel_id=1, source_target_pairs={{0,3},{1,2},{2,1},{3,0},{4,7},{5,6},{6,5},{7,4},{8,11},{9,10},{10,... | collective-permute-start | bytes 6152 | tf_op jit(solution)/shard_map/ppermute | solution.py:21
  27.4 3.6 %collective-permute-start.7 = (f32[1,512]{1,0:T(1,128)S(1)}, f32[1,512]{1,0:T(1,128)S(1)}, u32[]{:S(2)}, u32[]{:S(2)}) collective-permute-start(f32[1,512]{1,0:T(1,128)S(1)} %get-tuple-element.20), channel_id=1, source_target_pairs={{4,0},{5,1},{6,2},{7,3},{8,4},{9,5},{10,6},{11,7},{12,8},{13,9},{1... | collective-permute-start | bytes 6152 | tf_op jit(solution)/shard_map/ppermute | solution.py:50

commit v4 on v3

--- a/solution.py
+++ b/solution.py
@@ -193,27 +193,34 @@
         pl.when(hit & ~several)(functools.partial(add, *pair))
 
 
-def cross_kernel(cross_ref, behind_ref, back_in, to_cross, back):
+def cross_kernel(cross_ref, behind_ref, to_partner_in, back_in, to_chip, back):
     cross, behind = ids_of(cross_ref), ids_of(behind_ref, behind=True)
-    to_cross[...] = jnp.full_like(to_cross, LOW)
+    to_chip[0:1, :] = to_partner_in[...]
+    to_chip[1:2, :] = jnp.full_like(to_partner_in, LOW)
     back[...] = back_in[...]
 
     @pl.when(shares(cross, behind))
     def _():
         sims = product(rows_of(cross_ref), rows_of(behind_ref))
         back[...] = jnp.maximum(back[...], column_best(cross, behind, sims))
-        to_cross[...] = row_best(cross, behind, sims)
-
-
-def join_kernel(*refs):
-    *lines, best = refs
-    best[...] = jnp.maximum(functools.reduce(jnp.maximum, [line[...] for line in lines]), -1.0)
+        to_chip[1:2, :] = row_best(cross, behind, sims)
+
+
+def hand_on_kernel(to_mate, from_chip, out):
+    out[...] = jnp.maximum(to_mate[...], from_chip[1:2, :])
+
+
+def join_kernel(best_in, from_chip, from_mate, from_next, best):
+    near = jnp.maximum(best_in[...], from_chip[0:1, :])
+    far = jnp.maximum(from_mate[...], from_next[...])
+    best[...] = jnp.maximum(jnp.maximum(near, far), -1.0)
 
 
 def local(embeddings, block_cluster):
     rows, depth = embeddings.shape
     vmem = pl.BlockSpec(memory_space=pltpu.VMEM)
     line = jax.ShapeDtypeStruct((1, rows), jnp.float32)
+    lines = jax.ShapeDtypeStruct((2, rows), jnp.float32)
 
     def call(kernel, products, outs, specs, inputs, scratch=(), limit=16):
         return pl.pallas_call(
@@ -251,13 +258,17 @@
     best, to_mate, to_partner, back = call(
         behind_kernel, 3, (line,) * 4, [], (packet, mate, partner, behind, best)
     )
-    to_cross, back = call(cross_kernel, 1, (line, line), [], (cross, behind, back))
+    to_chip, back = call(
+        cross_kernel, 1, (lines, line), [], (cross, behind, to_partner, back)
+    )
     from_next = backward(back)
     if lax.axis_size("parts") % 2:
         from_next = jnp.where(ends()[1], from_next, LOW)
-    returned = (swapped(to_cross, 3), swapped(to_partner, 2), swapped(to_mate, 1), from_next)
+    from_chip = swapped(to_chip, 2)
     (best,) = call(near_kernel, 1, (line,), [], (packet, cross, best))
-    (best,) = call(join_kernel, 0, (line,), [], (best, *returned))
+    (to_mate,) = call(hand_on_kernel, 0, (line,), [], (to_mate, from_chip))
+    from_mate = swapped(to_mate, 1)
+    (best,) = call(join_kernel, 0, (line,), [], (best, from_chip, from_mate, from_next))
     return best.reshape(rows)
 
 

time: 31.8 us -> 31 us (0.975)
  starting transfers between devices: 8.37 us -> 7.64 us
  Pallas kernels: 4.11 us -> 4.73 us
  waiting for transfers between devices: 19.1 us -> 18.5 us
    ppermute x1, waiting for transfers between devices: 1.93 us -> 0.7 us  [backward(): lax.ppermute(array, ('parts', 'shift'), [(b, a) for a, b in next_quad()])]
    ppermute x6 -> x5, starting transfers between devices: 5.3 us -> 4.57 us  [swapped(): return lax.ppermute(array, 'shift', [(i, i ^ mask) for i in range(length)])]
    ppermute x6 -> x5, waiting for transfers between devices: 15.9 us -> 16.5 us  [swapped(): return lax.ppermute(array, 'shift', [(i, i ^ mask) for i in range(length)])]
    pallas_call x7 -> x8, Pallas kernels: 4.11 us -> 4.73 us  [call(): pl.pallas_call(kernel, out_shape=outs, in_specs=specs + [vmem] * (len(inp...]
  transfers between devices with their start and end apart: 8 -> 7, of which waited for: 3 -> 4; matrix products, arithmetic and copies ran while one was open for 0% -> 0% of each run, Pallas kernels for 7% -> 9%
where the time goes in v4:
time: 31 us; the launch traced here: 30.9 us
  waiting for transfers between devices  18.5 us (60%)
  starting transfers between devices  7.64 us (25%)
  Pallas kernels  4.73 us (15%)
    ppermute x5, waiting for transfers between devices, swapped(): return lax.ppermute(array, 'shift', [(i, i ^ mask) for i in range(length)])  16.5 us
    pallas_call x8, Pallas kernels, call(): pl.pallas_call(kernel, out_shape=outs, in_specs=specs + [vmem] * (len(inp...  4.73 us
    ppermute x5, starting transfers between devices, swapped(): return lax.ppermute(array, 'shift', [(i, i ^ mask) for i in range(length)])  4.57 us
    ppermute x1, starting transfers between devices, forward(): return lax.ppermute(array, ('parts', 'shift'), next_quad())  1.58 us
    ppermute x1, starting transfers between devices, backward(): lax.ppermute(array, ('parts', 'shift'), [(b, a) for a, b in next_quad()])  1.49 us
    ppermute x1, waiting for transfers between devices, forward(): return lax.ppermute(array, ('parts', 'shift'), next_quad())  1.25 us
    ppermute x1, waiting for transfers between devices, backward(): lax.ppermute(array, ('parts', 'shift'), [(b, a) for a, b in next_quad()])  0.7 us
  transfers between devices with their start and end apart: 7, of which 4 were waited for; matrix products, arithmetic and copies ran while one was open for 0% of the time, Pallas kernels for 9%

profile of v4, /device:TPU:0, one launch (start us, length us, event | category | flops | bytes accessed | tf_op | source)
XLA Modules:
  0.0 30.9 jit_solution(11074012110337504605)
XLA Ops:
  0.0 1.4 %shard_map.28.own_ref = bf16[528,768]{1,0:T(8,128)(2,1)S(1)} custom-call(s32[4]{0:T(128)} %ids_hbm.1, bf16[512,768]{1,0:T(8,128)(2,1)} %own_hbm.1), custom_call_target="tpu_custom_call" | custom-call | bytes 786432 | tf_op jit(solution)/shard_map/pallas_call | solution.py:226
  1.4 3.0 %collective-permute-start = (bf16[528,768]{1,0:T(8,128)(2,1)S(1)}, bf16[528,768]{1,0:T(8,128)(2,1)S(1)}, u32[]{:S(2)}, u32[]{:S(2)}) collective-permute-start(bf16[528,768]{1,0:T(8,128)(2,1)S(1)} %shard_map.28.own_ref), channel_id=1, source_target_pairs={{0,2},{1,3},{2,0},{3,1},{4,6},{5,7},{6,4},{7,5},{8,10},{9,11},{10,... | collective-permute-start | bytes 2433032 | tf_op jit(solution)/shard_map/ppermute | solution.py:21
  4.4 0.0 collective-permute-start.2
  4.4 1.6 %collective-permute-start.3 = (bf16[528,768]{1,0:T(8,128)(2,1)S(1)}, bf16[528,768]{1,0:T(8,128)(2,1)S(1)}, u32[]{:S(2)}, u32[]{:S(2)}) collective-permute-start(bf16[528,768]{1,0:T(8,128)(2,1)S(1)} %shard_map.28.own_ref), channel_id=1, source_target_pairs={{0,4},{1,5},{2,6},{3,7},{4,8},{5,9},{6,10},{7,11},{8,12},{9,13},{1... | collective-permute-start | bytes 2433032 | tf_op jit(solution)/shard_map/ppermute | solution.py:46
  6.0 0.6 %shard_map.29.refs_2_ = f32[1,512]{1,0:T(1,128)S(1)} custom-call(bf16[528,768]{1,0:T(8,128)(2,1)S(1)} %shard_map.28.own_ref), custom_call_target="tpu_custom_call" | custom-call | bytes 786432 | tf_op jit(solution)/shard_map/pallas_call | solution.py:226
  6.6 15.9 %collective-permute-done.refs_0_.partner_ref = bf16[528,768]{1,0:T(8,128)(2,1)S(1)} collective-permute-done((bf16[528,768]{1,0:T(8,128)(2,1)S(1)}, bf16[528,768]{1,0:T(8,128)(2,1)S(1)}, u32[]{:S(2)}, u32[]{:S(2)}) %collective-permute-start) | collective-permute-done | bytes 811040 | tf_op jit(solution)/shard_map/ppermute | solution.py:21
  22.5 0.0 collective-permute-start.1
  22.5 0.0 collective-permute-done.2.refs_1_.mate_ref
  22.5 1.2 %shard_map.30.best_in = f32[1,512]{1,0:T(1,128)S(1)} custom-call(bf16[528,768]{1,0:T(8,128)(2,1)S(1)} %shard_map.28.own_ref, bf16[528,768]{1,0:T(8,128)(2,1)S(1)} %collective-permute-done.refs_0_.partner_ref, bf16[528,768]{1,0:T(8,128)(2,1)S(1)} %collective-permute-done.2.refs_1_.mate_ref, f32[1,512]{1,0:T(1,128)S(1)} %shard_map.29.refs_2_), custom_call_target="tpu_custom_call" | custom-call | bytes 786432 | tf_op jit(solution)/shard_map/pallas_call | solution.py:226
  23.6 1.2 %collective-permute-done.3.behind_ref = bf16[528,768]{1,0:T(8,128)(2,1)S(1)} collective-permute-done((bf16[528,768]{1,0:T(8,128)(2,1)S(1)}, bf16[528,768]{1,0:T(8,128)(2,1)S(1)}, u32[]{:S(2)}, u32[]{:S(2)}) %collective-permute-start.3) | collective-permute-done | bytes 811040 | tf_op jit(solution)/shard_map/ppermute | solution.py:46
  24.9 0.1 shard_map.31
  25.0 0.0 collective-permute-done.1.refs_0_.cross_ref
  25.1 0.1 shard_map.33
  25.2 1.5 %collective-permute-start.4 = (f32[2,512]{1,0:T(2,128)S(1)}, f32[2,512]{1,0:T(2,128)S(1)}, u32[]{:S(2)}, u32[]{:S(2)}) collective-permute-start(f32[2,512]{1,0:T(2,128)S(1)} %get-tuple-element.18), channel_id=1, source_target_pairs={{0,2},{1,3},{2,0},{3,1},{4,6},{5,7},{6,4},{7,5},{8,10},{9,11},{10,... | collective-permute-start | bytes 12296 | tf_op jit(solution)/shard_map/ppermute | solution.py:21
  26.7 1.5 %collective-permute-start.6 = (f32[1,512]{1,0:T(1,128)S(1)}, f32[1,512]{1,0:T(1,128)S(1)}, u32[]{:S(2)}, u32[]{:S(2)}) collective-permute-start(f32[1,512]{1,0:T(1,128)S(1)} %get-tuple-element.20), channel_id=1, source_target_pairs={{4,0},{5,1},{6,2},{7,3},{8,4},{9,5},{10,6},{11,7},{12,8},{13,9},{1... | collective-permute-start | bytes 6152 | tf_op jit(solution)/shard_map/ppermute | solution.py:50
  28.2 0.6 %collective-permute-done.4.from_chip = f32[2,512]{1,0:T(2,128)S(1)} collective-permute-done((f32[2,512]{1,0:T(2,128)S(1)}, f32[2,512]{1,0:T(2,128)S(1)}, u32[]{:S(2)}, u32[]{:S(2)}) %collective-permute-start.4) | collective-permute-done | bytes 4128 | tf_op jit(solution)/shard_map/ppermute | solution.py:21
  28.9 0.0 collective-permute-start.5
  28.9 0.7 %shard_map.32.best_in = f32[1,512]{1,0:T(1,128)S(1)} custom-call(bf16[528,768]{1,0:T(8,128)(2,1)S(1)} %shard_map.28.own_ref, bf16[528,768]{1,0:T(8,128)(2,1)S(1)} %collective-permute-done.1.refs_0_.cross_ref, f32[1,512]{1,0:T(1,128)S(1)} %get-tuple-element.15.refs_1_), custom_call_target="tpu_custom_call" | custom-call | flops 402653184 | bytes 786432 | tf_op jit(solution)/shard_map/pallas_call | solution.py:226
  29.6 0.7 %collective-permute-done.6.from_next = f32[1,512]{1,0:T(1,128)S(1)} collective-permute-done((f32[1,512]{1,0:T(1,128)S(1)}, f32[1,512]{1,0:T(1,128)S(1)}, u32[]{:S(2)}, u32[]{:S(2)}) %collective-permute-start.6) | collective-permute-done | bytes 2080 | tf_op jit(solution)/shard_map/ppermute | solution.py:50
  30.3 0.0 collective-permute-done.5.from_mate
  30.3 0.6 %shard_map.35 = f32[1,512]{1,0:T(1,128)} custom-call(f32[1,512]{1,0:T(1,128)S(1)} %shard_map.32.best_in, f32[2,512]{1,0:T(2,128)S(1)} %collective-permute-done.4.from_chip, f32[1,512]{1,0:T(1,128)S(1)} %collective-permute-done.5.from_mate, f32[1,512]{1,0:T(1,128)S(1)} %collective-permute-done.6.from_next), custom_call_target="tpu_custom_call" | custom-call | bytes 786432 | tf_op jit(solution)/shard_map/pallas_call | solution.py:226
  (1 shorter events, 0.0 us)
Async XLA Ops:
  1.4 21.1 %collective-permute-start = (bf16[528,768]{1,0:T(8,128)(2,1)S(1)}, bf16[528,768]{1,0:T(8,128)(2,1)S(1)}, u32[]{:S(2)}, u32[]{:S(2)}) collective-permute-start(bf16[528,768]{1,0:T(8,128)(2,1)S(1)} %shard_map.28.own_ref), channel_id=1, source_target_pairs={{0,2},{1,3},{2,0},{3,1},{4,6},{5,7},{6,4},{7,5},{8,10},{9,11},{10,... | collective-permute-start | bytes 2433032 | tf_op jit(solution)/shard_map/ppermute | solution.py:21
  4.4 18.1 %collective-permute-start.2 = (bf16[528,768]{1,0:T(8,128)(2,1)S(1)}, bf16[528,768]{1,0:T(8,128)(2,1)S(1)}, u32[]{:S(2)}, u32[]{:S(2)}) collective-permute-start(bf16[528,768]{1,0:T(8,128)(2,1)S(1)} %shard_map.28.own_ref), channel_id=1, source_target_pairs={{0,1},{1,0},{2,3},{3,2},{4,5},{5,4},{6,7},{7,6},{8,9},{9,8},{10,11... | collective-permute-start | bytes 2433032 | tf_op jit(solution)/shard_map/ppermute | solution.py:21
  4.4 20.5 %collective-permute-start.3 = (bf16[528,768]{1,0:T(8,128)(2,1)S(1)}, bf16[528,768]{1,0:T(8,128)(2,1)S(1)}, u32[]{:S(2)}, u32[]{:S(2)}) collective-permute-start(bf16[528,768]{1,0:T(8,128)(2,1)S(1)} %shard_map.28.own_ref), channel_id=1, source_target_pairs={{0,4},{1,5},{2,6},{3,7},{4,8},{5,9},{6,10},{7,11},{8,12},{9,13},{1... | collective-permute-start | bytes 2433032 | tf_op jit(solution)/shard_map/ppermute | solution.py:46
  22.5 2.6 %collective-permute-start.1 = (bf16[528,768]{1,0:T(8,128)(2,1)S(1)}, bf16[528,768]{1,0:T(8,128)(2,1)S(1)}, u32[]{:S(2)}, u32[]{:S(2)}) collective-permute-start(bf16[528,768]{1,0:T(8,128)(2,1)S(1)} %collective-permute-done.refs_0_.partner_ref), channel_id=1, source_target_pairs={{0,1},{1,0},{2,3},{3,2},{4,5},{5,4},{6,7},{7,6},{8,9},{9,8},{10,11... | collective-permute-start | bytes 2433032 | tf_op jit(solution)/shard_map/ppermute | solution.py:21
  25.2 3.7 %collective-permute-start.4 = (f32[2,512]{1,0:T(2,128)S(1)}, f32[2,512]{1,0:T(2,128)S(1)}, u32[]{:S(2)}, u32[]{:S(2)}) collective-permute-start(f32[2,512]{1,0:T(2,128)S(1)} %get-tuple-element.18), channel_id=1, source_target_pairs={{0,2},{1,3},{2,0},{3,1},{4,6},{5,7},{6,4},{7,5},{8,10},{9,11},{10,... | collective-permute-start | bytes 12296 | tf_op jit(solution)/shard_map/ppermute | solution.py:21
  26.7 3.6 %collective-permute-start.6 = (f32[1,512]{1,0:T(1,128)S(1)}, f32[1,512]{1,0:T(1,128)S(1)}, u32[]{:S(2)}, u32[]{:S(2)}) collective-permute-start(f32[1,512]{1,0:T(1,128)S(1)} %get-tuple-element.20), channel_id=1, source_target_pairs={{4,0},{5,1},{6,2},{7,3},{8,4},{9,5},{10,6},{11,7},{12,8},{13,9},{1... | collective-permute-start | bytes 6152 | tf_op jit(solution)/shard_map/ppermute | solution.py:50
  28.9 1.4 %collective-permute-start.5 = (f32[1,512]{1,0:T(1,128)S(1)}, f32[1,512]{1,0:T(1,128)S(1)}, u32[]{:S(2)}, u32[]{:S(2)}) collective-permute-start(f32[1,512]{1,0:T(1,128)S(1)} %shard_map.34), channel_id=1, source_target_pairs={{0,1},{1,0},{2,3},{3,2},{4,5},{5,4},{6,7},{7,6},{8,9},{9,8},{10,11... | collective-permute-start | bytes 6152 | tf_op jit(solution)/shard_map/ppermute | solution.py:21

commit v5 on v4

--- a/solution.py
+++ b/solution.py
@@ -1,4 +1,5 @@
 import functools
+import itertools
 import math
 
 import jax
@@ -182,15 +183,17 @@
         back[...] = jnp.maximum(back[...], column_best(ids, behind, sims))
         out[...] = jnp.maximum(out[...], row_best(ids, behind, sims))
 
-    several = (hits[0] & hits[1]) | (hits[0] & hits[2]) | (hits[1] & hits[2])
-
-    @pl.when(several)
-    def _():
-        for pair in pairs:
-            add(*pair)
-
-    for hit, pair in zip(hits, pairs):
-        pl.when(hit & ~several)(functools.partial(add, *pair))
+    for due in itertools.product((False, True), repeat=len(pairs)):
+        if any(due):
+            exact = functools.reduce(
+                jnp.logical_and, [hit if wanted else ~hit for hit, wanted in zip(hits, due)]
+            )
+
+            @pl.when(exact)
+            def _(due=due):
+                for wanted, pair in zip(due, pairs):
+                    if wanted:
+                        add(*pair)
 
 
 def cross_kernel(cross_ref, behind_ref, to_partner_in, back_in, to_chip, back):

time: 31 us -> 31.2 us (level)
  waiting for transfers between devices: 18.5 us -> 19.7 us
  Pallas kernels: 4.73 us -> 3.73 us
    pallas_call x8, Pallas kernels: 4.73 us -> 3.73 us  [call(): pl.pallas_call(kernel, out_shape=outs, in_specs=specs + [vmem] * (len(inp...]
    ppermute x1, waiting for transfers between devices: 0.7 us -> 1.52 us  [backward(): lax.ppermute(array, ('parts', 'shift'), [(b, a) for a, b in next_quad()])]
    ppermute x1, waiting for transfers between devices: 1.25 us -> 1.66 us  [forward(): return lax.ppermute(array, ('parts', 'shift'), next_quad())]
  transfers between devices with their start and end apart: 7 -> 7, of which waited for: 4 -> 4; matrix products, arithmetic and copies ran while one was open for 0% -> 0% of each run, Pallas kernels for 9% -> 5%
where the time goes in v5:
time: 31.2 us; the launch traced here: 31.1 us
  waiting for transfers between devices  19.7 us (63%)
  starting transfers between devices  7.62 us (24%)
  Pallas kernels  3.73 us (12%)
    ppermute x5, waiting for transfers between devices, swapped(): return lax.ppermute(array, 'shift', [(i, i ^ mask) for i in range(length)])  16.5 us
    ppermute x5, starting transfers between devices, swapped(): return lax.ppermute(array, 'shift', [(i, i ^ mask) for i in range(length)])  4.56 us
    pallas_call x8, Pallas kernels, call(): pl.pallas_call(kernel, out_shape=outs, in_specs=specs + [vmem] * (len(inp...  3.73 us
    ppermute x1, waiting for transfers between devices, forward(): return lax.ppermute(array, ('parts', 'shift'), next_quad())  1.66 us
    ppermute x1, starting transfers between devices, forward(): return lax.ppermute(array, ('parts', 'shift'), next_quad())  1.58 us
    ppermute x1, waiting for transfers between devices, backward(): lax.ppermute(array, ('parts', 'shift'), [(b, a) for a, b in next_quad()])  1.52 us
    ppermute x1, starting transfers between devices, backward(): lax.ppermute(array, ('parts', 'shift'), [(b, a) for a, b in next_quad()])  1.49 us
  transfers between devices with their start and end apart: 7, of which 4 were waited for; matrix products, arithmetic and copies ran while one was open for 0% of the time, Pallas kernels for 5%

profile of v5, /device:TPU:0, one launch (start us, length us, event | category | flops | bytes accessed | tf_op | source)
XLA Modules:
  0.0 31.1 jit_solution(3988409180568008567)
XLA Ops:
  0.0 1.4 %shard_map.28.own_ref = bf16[528,768]{1,0:T(8,128)(2,1)S(1)} custom-call(s32[4]{0:T(128)} %ids_hbm.1, bf16[512,768]{1,0:T(8,128)(2,1)} %own_hbm.1), custom_call_target="tpu_custom_call" | custom-call | bytes 786432 | tf_op jit(solution)/shard_map/pallas_call | solution.py:229
  1.4 3.0 %collective-permute-start = (bf16[528,768]{1,0:T(8,128)(2,1)S(1)}, bf16[528,768]{1,0:T(8,128)(2,1)S(1)}, u32[]{:S(2)}, u32[]{:S(2)}) collective-permute-start(bf16[528,768]{1,0:T(8,128)(2,1)S(1)} %shard_map.28.own_ref), channel_id=1, source_target_pairs={{0,2},{1,3},{2,0},{3,1},{4,6},{5,7},{6,4},{7,5},{8,10},{9,11},{10,... | collective-permute-start | bytes 2433032 | tf_op jit(solution)/shard_map/ppermute | solution.py:22
  4.4 0.0 collective-permute-start.2
  4.4 1.6 %collective-permute-start.3 = (bf16[528,768]{1,0:T(8,128)(2,1)S(1)}, bf16[528,768]{1,0:T(8,128)(2,1)S(1)}, u32[]{:S(2)}, u32[]{:S(2)}) collective-permute-start(bf16[528,768]{1,0:T(8,128)(2,1)S(1)} %shard_map.28.own_ref), channel_id=1, source_target_pairs={{0,4},{1,5},{2,6},{3,7},{4,8},{5,9},{6,10},{7,11},{8,12},{9,13},{1... | collective-permute-start | bytes 2433032 | tf_op jit(solution)/shard_map/ppermute | solution.py:47
  6.0 0.6 %shard_map.29.refs_2_ = f32[1,512]{1,0:T(1,128)S(1)} custom-call(bf16[528,768]{1,0:T(8,128)(2,1)S(1)} %shard_map.28.own_ref), custom_call_target="tpu_custom_call" | custom-call | bytes 786432 | tf_op jit(solution)/shard_map/pallas_call | solution.py:229
  6.6 15.9 %collective-permute-done.refs_0_.partner_ref = bf16[528,768]{1,0:T(8,128)(2,1)S(1)} collective-permute-done((bf16[528,768]{1,0:T(8,128)(2,1)S(1)}, bf16[528,768]{1,0:T(8,128)(2,1)S(1)}, u32[]{:S(2)}, u32[]{:S(2)}) %collective-permute-start) | collective-permute-done | bytes 811040 | tf_op jit(solution)/shard_map/ppermute | solution.py:22
  22.5 0.0 collective-permute-start.1
  22.5 0.0 collective-permute-done.2.refs_1_.mate_ref
  22.5 0.7 %shard_map.30.best_in = f32[1,512]{1,0:T(1,128)S(1)} custom-call(bf16[528,768]{1,0:T(8,128)(2,1)S(1)} %shard_map.28.own_ref, bf16[528,768]{1,0:T(8,128)(2,1)S(1)} %collective-permute-done.refs_0_.partner_ref, bf16[528,768]{1,0:T(8,128)(2,1)S(1)} %collective-permute-done.2.refs_1_.mate_ref, f32[1,512]{1,0:T(1,128)S(1)} %shard_map.29.refs_2_), custom_call_target="tpu_custom_call" | custom-call | bytes 786432 | tf_op jit(solution)/shard_map/pallas_call | solution.py:229
  23.2 1.7 %collective-permute-done.3.behind_ref = bf16[528,768]{1,0:T(8,128)(2,1)S(1)} collective-permute-done((bf16[528,768]{1,0:T(8,128)(2,1)S(1)}, bf16[528,768]{1,0:T(8,128)(2,1)S(1)}, u32[]{:S(2)}, u32[]{:S(2)}) %collective-permute-start.3) | collective-permute-done | bytes 811040 | tf_op jit(solution)/shard_map/ppermute | solution.py:47
  24.9 0.2 shard_map.31
  25.1 0.0 collective-permute-done.1.refs_0_.cross_ref
  25.1 0.1 shard_map.33
  25.2 1.5 %collective-permute-start.4 = (f32[2,512]{1,0:T(2,128)S(1)}, f32[2,512]{1,0:T(2,128)S(1)}, u32[]{:S(2)}, u32[]{:S(2)}) collective-permute-start(f32[2,512]{1,0:T(2,128)S(1)} %get-tuple-element.18), channel_id=1, source_target_pairs={{0,2},{1,3},{2,0},{3,1},{4,6},{5,7},{6,4},{7,5},{8,10},{9,11},{10,... | collective-permute-start | bytes 12296 | tf_op jit(solution)/shard_map/ppermute | solution.py:22
  26.7 1.5 %collective-permute-start.6 = (f32[1,512]{1,0:T(1,128)S(1)}, f32[1,512]{1,0:T(1,128)S(1)}, u32[]{:S(2)}, u32[]{:S(2)}) collective-permute-start(f32[1,512]{1,0:T(1,128)S(1)} %get-tuple-element.20), channel_id=1, source_target_pairs={{4,0},{5,1},{6,2},{7,3},{8,4},{9,5},{10,6},{11,7},{12,8},{13,9},{1... | collective-permute-start | bytes 6152 | tf_op jit(solution)/shard_map/ppermute | solution.py:51
  28.2 0.7 %collective-permute-done.4.from_chip = f32[2,512]{1,0:T(2,128)S(1)} collective-permute-done((f32[2,512]{1,0:T(2,128)S(1)}, f32[2,512]{1,0:T(2,128)S(1)}, u32[]{:S(2)}, u32[]{:S(2)}) %collective-permute-start.4) | collective-permute-done | bytes 4128 | tf_op jit(solution)/shard_map/ppermute | solution.py:22
  28.9 0.0 collective-permute-start.5
  28.9 0.1 shard_map.32.best_in
  29.0 1.5 %collective-permute-done.6.from_next = f32[1,512]{1,0:T(1,128)S(1)} collective-permute-done((f32[1,512]{1,0:T(1,128)S(1)}, f32[1,512]{1,0:T(1,128)S(1)}, u32[]{:S(2)}, u32[]{:S(2)}) %collective-permute-start.6) | collective-permute-done | bytes 2080 | tf_op jit(solution)/shard_map/ppermute | solution.py:51
  30.5 0.0 collective-permute-done.5.from_mate
  30.6 0.6 %shard_map.35 = f32[1,512]{1,0:T(1,128)} custom-call(f32[1,512]{1,0:T(1,128)S(1)} %shard_map.32.best_in, f32[2,512]{1,0:T(2,128)S(1)} %collective-permute-done.4.from_chip, f32[1,512]{1,0:T(1,128)S(1)} %collective-permute-done.5.from_mate, f32[1,512]{1,0:T(1,128)S(1)} %collective-permute-done.6.from_next), custom_call_target="tpu_custom_call" | custom-call | bytes 786432 | tf_op jit(solution)/shard_map/pallas_call | solution.py:229
  (1 shorter events, 0.0 us)
Async XLA Ops:
  1.4 21.1 %collective-permute-start = (bf16[528,768]{1,0:T(8,128)(2,1)S(1)}, bf16[528,768]{1,0:T(8,128)(2,1)S(1)}, u32[]{:S(2)}, u32[]{:S(2)}) collective-permute-start(bf16[528,768]{1,0:T(8,128)(2,1)S(1)} %shard_map.28.own_ref), channel_id=1, source_target_pairs={{0,2},{1,3},{2,0},{3,1},{4,6},{5,7},{6,4},{7,5},{8,10},{9,11},{10,... | collective-permute-start | bytes 2433032 | tf_op jit(solution)/shard_map/ppermute | solution.py:22
  4.4 18.1 %collective-permute-start.2 = (bf16[528,768]{1,0:T(8,128)(2,1)S(1)}, bf16[528,768]{1,0:T(8,128)(2,1)S(1)}, u32[]{:S(2)}, u32[]{:S(2)}) collective-permute-start(bf16[528,768]{1,0:T(8,128)(2,1)S(1)} %shard_map.28.own_ref), channel_id=1, source_target_pairs={{0,1},{1,0},{2,3},{3,2},{4,5},{5,4},{6,7},{7,6},{8,9},{9,8},{10,11... | collective-permute-start | bytes 2433032 | tf_op jit(solution)/shard_map/ppermute | solution.py:22
  4.4 20.5 %collective-permute-start.3 = (bf16[528,768]{1,0:T(8,128)(2,1)S(1)}, bf16[528,768]{1,0:T(8,128)(2,1)S(1)}, u32[]{:S(2)}, u32[]{:S(2)}) collective-permute-start(bf16[528,768]{1,0:T(8,128)(2,1)S(1)} %shard_map.28.own_ref), channel_id=1, source_target_pairs={{0,4},{1,5},{2,6},{3,7},{4,8},{5,9},{6,10},{7,11},{8,12},{9,13},{1... | collective-permute-start | bytes 2433032 | tf_op jit(solution)/shard_map/ppermute | solution.py:47
  22.5 2.6 %collective-permute-start.1 = (bf16[528,768]{1,0:T(8,128)(2,1)S(1)}, bf16[528,768]{1,0:T(8,128)(2,1)S(1)}, u32[]{:S(2)}, u32[]{:S(2)}) collective-permute-start(bf16[528,768]{1,0:T(8,128)(2,1)S(1)} %collective-permute-done.refs_0_.partner_ref), channel_id=1, source_target_pairs={{0,1},{1,0},{2,3},{3,2},{4,5},{5,4},{6,7},{7,6},{8,9},{9,8},{10,11... | collective-permute-start | bytes 2433032 | tf_op jit(solution)/shard_map/ppermute | solution.py:22
  25.2 3.7 %collective-permute-start.4 = (f32[2,512]{1,0:T(2,128)S(1)}, f32[2,512]{1,0:T(2,128)S(1)}, u32[]{:S(2)}, u32[]{:S(2)}) collective-permute-start(f32[2,512]{1,0:T(2,128)S(1)} %get-tuple-element.18), channel_id=1, source_target_pairs={{0,2},{1,3},{2,0},{3,1},{4,6},{5,7},{6,4},{7,5},{8,10},{9,11},{10,... | collective-permute-start | bytes 12296 | tf_op jit(solution)/shard_map/ppermute | solution.py:22
  26.7 3.8 %collective-permute-start.6 = (f32[1,512]{1,0:T(1,128)S(1)}, f32[1,512]{1,0:T(1,128)S(1)}, u32[]{:S(2)}, u32[]{:S(2)}) collective-permute-start(f32[1,512]{1,0:T(1,128)S(1)} %get-tuple-element.20), channel_id=1, source_target_pairs={{4,0},{5,1},{6,2},{7,3},{8,4},{9,5},{10,6},{11,7},{12,8},{13,9},{1... | collective-permute-start | bytes 6152 | tf_op jit(solution)/shard_map/ppermute | solution.py:51
  28.9 1.7 %collective-permute-start.5 = (f32[1,512]{1,0:T(1,128)S(1)}, f32[1,512]{1,0:T(1,128)S(1)}, u32[]{:S(2)}, u32[]{:S(2)}) collective-permute-start(f32[1,512]{1,0:T(1,128)S(1)} %shard_map.34), channel_id=1, source_target_pairs={{0,1},{1,0},{2,3},{3,2},{4,5},{5,4},{6,7},{7,6},{8,9},{9,8},{10,11... | collective-permute-start | bytes 6152 | tf_op jit(solution)/shard_map/ppermute | solution.py:22
